TPU v7x, 32 devices: a whole 2x2x4 slice. The times are simulated.
32 devices in a mesh: band: 4 (over z), grid: 8 (over y, x, core).
Axes of the slice: x: 2, y: 2, z: 4, core: 2. Of those that a mesh axis runs over, the one named last changes fastest.
Arguments:
- orbitals: float32 [16, 96, 9216], P('band', 'grid'), may hold values from -6 to 6
- pair_mask: int32 [16, 4], P('band'), may hold values 0 or 1
- cycle_step: int32 [], replicated, may hold values from 1 to 3
Outputs:
- exchange_field: float32 [16, 96, 9216], P('band', 'grid')
- projection: float32 [16, 4], P('band')
All inputs are finite; a program needn't handle non-finite values. No bound on the sum of `pair_mask` on one device may be relied on, other than what follows from the above.
Results may differ from a plain program's by a relative error of at most 0.0003.
Values sent between devices are 32-bit elements; how exact they have to be, the bound alone decides.
No kernel may reach another device: no remote copies, remote signals or barrier semaphores. Data moves between devices by JAX's collectives and lax.ppermute only.
A program may use at most 192 MiB of HBM per device.

v0:
```python
import math

import jax
import jax.numpy as jnp
from jax import lax
from jax.sharding import PartitionSpec as P

NX = 96
NY = 96
NZ = 96


box_length = 16.0
highest = lax.Precision.HIGHEST


def passed_along(block, axis, distance):
    devices = range(lax.axis_size(axis))
    route = [((i - distance) % len(devices), i) for i in devices]
    return lax.ppermute(block, axis, route)


def hartley_table(length):
    index = jnp.arange(length, dtype=jnp.int32)
    product = index[:, None] * index[None, :] % length
    angle = product.astype(jnp.float32) * (2.0 * math.pi / length)
    return jnp.cos(angle) + jnp.sin(angle)


def folded(index, length):
    return jnp.where(index * 2 >= length, index - length, index).astype(jnp.float32)


def across_planes(field, table_y, table_z):
    count = field.shape[0]
    planes = field.shape[1]
    shaped = field.reshape(count * planes * NY, NZ)
    shaped = jnp.matmul(shaped, table_z, precision=highest)
    shaped = shaped.reshape(count * planes, NY, NZ)
    shaped = jnp.matmul(table_y, shaped, precision=highest)
    return shaped.reshape(count, planes, NY * NZ)


def shards(orbitals, pair_mask, cycle_step):
    orbit_count = orbitals.shape[0]
    planes = orbitals.shape[1]
    grid_count = lax.axis_size("grid")
    slab_rows = NY // grid_count

    def one_hop(turn, block):
        return passed_along(block, "band", 1)

    visiting = lax.fori_loop(0, cycle_step, one_hop, orbitals)
    table_x = hartley_table(NX)
    table_y = hartley_table(NY)
    table_z = hartley_table(NZ)
    row_index = lax.axis_index("grid") * slab_rows + jnp.arange(slab_rows, dtype=jnp.int32)
    freq_x = folded(jnp.arange(NX, dtype=jnp.int32), NX)
    freq_y = folded(row_index, NY)
    freq_z = folded(jnp.arange(NZ, dtype=jnp.int32), NZ)
    squares = freq_x[:, None, None] ** 2 + freq_y[None, :, None] ** 2 + freq_z[None, None, :] ** 2
    coulomb = box_length * box_length / math.pi / (NX * NY * NZ)
    kernel = jnp.where(squares > 0.5, coulomb / jnp.maximum(squares, 1.0), jnp.float32(0.0))
    kernel = kernel.reshape(NX, slab_rows * NZ)

    def solve_items(spectra):
        along = jnp.matmul(table_x, spectra, precision=highest) * kernel
        along = jnp.matmul(table_x, along, precision=highest)
        return lax.all_to_all(along, "grid", split_axis=1, concat_axis=2, tiled=True)

    mask_float = pair_mask.astype(jnp.float32).reshape(
        orbit_count // orbit_count, orbit_count, orbit_count
    )
    own_rows = orbitals.reshape(orbit_count // orbit_count, orbit_count, planes, NY * NZ)

    def one_group(carry, inputs):
        rows, weights = inputs
        density = (rows[:, None] * visiting[None]).reshape(
            orbit_count * orbit_count, planes, NY * NZ
        )
        spectra = across_planes(density, table_y, table_z)
        potential = solve_items(
            lax.all_to_all(spectra, "grid", split_axis=2, concat_axis=1, tiled=True)
        )
        potential = across_planes(potential, table_y, table_z)
        potential = potential.reshape(orbit_count, orbit_count, planes, NY * NZ)
        field = -jnp.einsum("aj,ajxr->axr", weights, potential * visiting[None], precision=highest)
        return (carry, field)

    start_carry = jnp.zeros((), jnp.float32)
    _, fields = lax.scan(one_group, start_carry, (own_rows, mask_float))
    exchange_field = fields.reshape(orbit_count, planes, NY * NZ)
    local_terms = jnp.einsum("axr,cxr->ac", orbitals, exchange_field, precision=highest) / (
        NX * NY * NZ
    )
    projection = lax.psum(local_terms, "grid")
    return (exchange_field, projection)


def solution(mesh):
    return jax.shard_map(
        shards,
        mesh=mesh,
        in_specs=(P("band", "grid", None), P("band", None), P()),
        out_specs=(P("band", "grid", None), P("band", None)),
        check_vma=False,
    )
```

profile of v0, /device:TPU:0, one launch (start us, length us, event | category | flops | bytes accessed | tf_op | source)
XLA Modules:
  0.0 916.5 jit_solution(2581185637141054552)
XLA Ops:
  0.6 4.0 copy.18
  4.7 129.1 %while.3 = (s32[]{:T(128)}, f32[4,12,9216]{2,0,1:T(4,128)S(1)}, s32[]{:T(128)}, s32[]{:T(128)}) while((s32[]{:T(128)}, f32[4,12,9216]{2,0,1:T(4,128)S(1)}, s32[]{:T(128)}, s32[]{:T(128)}) %tuple.33), condition=%wide.region_1.0_spmd, body=%wide.region_0.0_spmd.sunk | while | flops 2 | bytes 10616925 | solution.py:53
  5.3 3.1 collective-permute-start
  8.4 40.6 %collective-permute-done = f32[4,12,9216]{2,0,1:T(4,128)S(1)} collective-permute-done((f32[4,12,9216]{2,0,1:T(4,128)S(1)}, f32[4,12,9216]{2,0,1:T(4,128)S(1)}, u32[]{:S(2)}, u32[]{:S(2)}) %collective-permute-start) | collective-permute-done | bytes 1769504 | tf_op jit(solution)/shard_map/while/body/ppermute | solution.py:20
  49.0 0.1 copy.51
  49.8 0.1 collective-permute-start
  49.9 41.6 %collective-permute-done = f32[4,12,9216]{2,0,1:T(4,128)S(1)} collective-permute-done((f32[4,12,9216]{2,0,1:T(4,128)S(1)}, f32[4,12,9216]{2,0,1:T(4,128)S(1)}, u32[]{:S(2)}, u32[]{:S(2)}) %collective-permute-start) | collective-permute-done | bytes 1769504 | tf_op jit(solution)/shard_map/while/body/ppermute | solution.py:20
  91.5 0.1 copy.51
  92.2 0.1 collective-permute-start
  92.3 40.7 %collective-permute-done = f32[4,12,9216]{2,0,1:T(4,128)S(1)} collective-permute-done((f32[4,12,9216]{2,0,1:T(4,128)S(1)}, f32[4,12,9216]{2,0,1:T(4,128)S(1)}, u32[]{:S(2)}, u32[]{:S(2)}) %collective-permute-start) | collective-permute-done | bytes 1769504 | tf_op jit(solution)/shard_map/while/body/ppermute | solution.py:20
  133.0 0.1 copy.51
  133.8 1.0 copy.19
  134.8 1.4 copy-done
  136.2 6.4 broadcast_multiply_fusion.1
  142.6 11.2 %mul.150 = f32[192,96,96]{2,1,0:T(8,128)} reshape(f32[4,4,12,9216]{3,2,1,0:T(8,128)} %broadcast_multiply_fusion.1) | data formatting | bytes 14155776 | tf_op jit(solution)/shard_map/while/body/eval_jaxpr/mul | solution.py:78
  153.8 23.7 %fusion.21 = f32[192,96,96]{1,2,0:T(8,128)S(1)} fusion(f32[192,96,96]{2,1,0:T(8,128)} %mul.150), kind=kOutput, calls=%fused_computation.30 | convolution fusion | flops 2038523904 | bytes 14155776 | tf_op jit(solution)/shard_map/while/body/eval_jaxpr/dot_general | solution.py:38
  177.5 10.4 %convolution_bitcast_fusion.1 = f32[192,96,96]{1,2,0:T(8,128)} fusion(f32[192,96,96]{1,2,0:T(8,128)S(1)} %fusion.21), kind=kOutput, calls=%fused_computation.11 | convolution fusion | flops 2038523904 | bytes 14155776 | tf_op jit(solution)/shard_map/while/body/eval_jaxpr/dot_general | solution.py:40
  187.9 12.5 %copy.37 = f32[192,96,96]{0,2,1:T(8,128)} copy(f32[192,96,96]{1,2,0:T(8,128)} %convolution_bitcast_fusion.1) | data formatting | bytes 14155776 | tf_op jit(solution)/shard_map/while/body/eval_jaxpr/reshape | solution.py:41
  200.4 49.7 %reshape.119 = f32[16,12,9216]{1,0,2:T(8,128)} reshape(f32[192,96,96]{0,2,1:T(8,128)} %copy.37) | data formatting | bytes 14155776 | tf_op jit(solution)/shard_map/while/body/eval_jaxpr/reshape | solution.py:41
  250.1 117.6 %reshape.120 = f32[8,1,221184]{2,1,0:T(1,128)} reshape(f32[9216,16,12]{2,1,0:T(8,128)} %bitcast.61) | data formatting | bytes 14155776
  367.7 5.0 all-to-all-start
  372.7 0.1 add.115
  372.8 0.1 broadcast_add_fusion
  372.9 0.2 fusion.12
  373.1 0.2 copy.26
  373.3 79.4 %all-to-all-done = f32[8,1,221184]{2,1,0:T(1,128)} async-done(((f32[8,1,221184]{2,1,0:T(1,128)}), f32[8,1,221184]{2,1,0:T(1,128)}, u32[]{:S(2)}, u32[]{:S(2)}) %all-to-all-start) | async-done | bytes 7077920 | tf_op jit(solution)/shard_map/while/body/eval_jaxpr/all_to_all | solution.py:83
  452.7 0.5 broadcast.140
  453.3 76.3 %reduce = f32[8,221184]{1,0:T(8,128)} reduce(f32[8,1,221184]{2,1,0:T(1,128)} %all-to-all-done, f32[]{:T(128)} %broadcast.140), dimensions={1}, to_apply=%all_to_all.39.reduce_sub_computation | reduce | bytes 14155780 | tf_op jit(solution)/shard_map/while/body/eval_jaxpr/all_to_all | solution.py:83
  529.6 114.7 %reshape.121 = f32[9216,16,12]{2,1,0:T(8,128)} reshape(f32[8,221184]{1,0:T(8,128)} %reduce) | data formatting | bytes 14155776
  644.3 44.3 %copy.24 = f32[16,8,12,1152]{3,0,2,1:T(8,128)} copy(f32[16,8,12,1152]{2,0,3,1:T(8,128)} %bitcast.4) | data formatting | bytes 14155776 | tf_op jit(solution)/shard_map/while/body/eval_jaxpr/all_to_all | solution.py:83
  688.6 11.2 %fusion.3 = f32[16,1152,96]{1,2,0:T(8,128)S(1)} fusion(f32[16,96,1152]{2,0,1:T(8,128)} %bitcast.70), kind=kOutput, calls=%fused_computation.4 | convolution fusion | flops 2038523904 | bytes 14155776 | tf_op jit(solution)/shard_map/while/body/eval_jaxpr/dot_general | solution.py:67
  699.8 7.4 fusion.5
  707.2 7.0 copy.27
  714.3 5.1 all-to-all-start.1
  719.4 80.0 %all-to-all-done.1 = f32[16,96,1152]{2,0,1:T(8,128)} async-done(((f32[16,96,1152]{2,0,1:T(8,128)}), f32[16,96,1152]{2,0,1:T(8,128)}, u32[]{:S(2)}, u32[]{:S(2)}) %all-to-all-start.1) | async-done | bytes 7077920 | tf_op jit(solution)/shard_map/while/body/eval_jaxpr/all_to_all | solution.py:69
  799.4 9.9 %copy.28 = f32[16,12,8,1152]{3,2,1,0:T(8,128)} copy(f32[16,12,8,1152]{3,0,1,2:T(8,128)} %bitcast.10) | data formatting | bytes 14155776 | tf_op jit(solution)/shard_map/while/body/eval_jaxpr/all_to_all | solution.py:69
  809.4 10.2 %dot_general.37 = f32[192,96,96]{2,1,0:T(8,128)} reshape(f32[16,12,8,1152]{3,2,1,0:T(8,128)} %copy.28) | data formatting | bytes 14155776 | tf_op jit(solution)/shard_map/while/body/eval_jaxpr/dot_general | solution.py:38
  819.6 23.7 %fusion.16 = f32[192,96,96]{1,2,0:T(8,128)S(1)} fusion(f32[192,96,96]{2,1,0:T(8,128)} %dot_general.37), kind=kOutput, calls=%fused_computation.25 | convolution fusion | flops 2038523904 | bytes 14155776 | tf_op jit(solution)/shard_map/while/body/eval_jaxpr/dot_general | solution.py:38
  843.2 10.5 %convolution_bitcast_fusion = f32[192,96,96]{1,2,0:T(8,128)} fusion(f32[192,96,96]{1,2,0:T(8,128)S(1)} %fusion.16), kind=kOutput, calls=%fused_computation.10 | convolution fusion | flops 2038523904 | bytes 14155776 | tf_op jit(solution)/shard_map/while/body/eval_jaxpr/dot_general | solution.py:40
  853.7 9.6 %copy.30 = f32[192,96,96]{2,1,0:T(8,128)} copy(f32[192,96,96]{1,2,0:T(8,128)} %convolution_bitcast_fusion) | data formatting | bytes 14155776 | tf_op jit(solution)/shard_map/while/body/eval_jaxpr/transpose | solution.py:40
  863.4 11.4 %reshape.114 = f32[4,4,12,9216]{3,2,1,0:T(8,128)} reshape(f32[192,96,96]{2,1,0:T(8,128)} %copy.30) | data formatting | bytes 14155776 | tf_op jit(solution)/shard_map/while/body/eval_jaxpr/reshape;while/body/eval_jaxpr/reshape | solution.py:86
  874.8 5.1 broadcast_multiply_fusion
  879.8 14.6 %fusion.1 = f32[4,1,12,9216]{3,1,2,0:T(1,128)S(1)} fusion(f32[4,4,1,1]{1,2,3,0:T(1,128)S(1)} %bitcast.71, f32[4,4,12,9216]{3,2,1,0:T(8,128)S(1)} %broadcast_multiply_fusion), kind=kOutput, calls=%fused_computation.2 | convolution fusion | flops 21233664 | bytes 8847424 | tf_op jit(solution)/shard_map/while/body/eval_jaxpr/aj,ajxr->axr/dot_general | solution.py:87
  894.5 1.3 bitcast_negate_fusion
  895.8 0.0 copy-start.3
  895.8 8.0 fusion.8
  903.7 11.8 %psum.7 = f32[4,4]{0,1:T(4,128)S(1)} all-reduce(f32[4,4]{0,1:T(4,128)S(1)} %fusion.8), channel_id=1, replica_groups=mesh['band'=4,'grid'=8] {'grid'}, use_global_device_ids=true, to_apply=%region_2.3 | all-reduce | flops 16 | bytes 128 | tf_op jit(solution)/shard_map/psum | solution.py:96
  915.5 0.7 copy.31
  (12 shorter events, 0.0 us)
Async XLA Ops:
  0.6 4.0 copy-start.2
  5.3 43.7 %collective-permute-start = (f32[4,12,9216]{2,0,1:T(4,128)S(1)}, f32[4,12,9216]{2,0,1:T(4,128)S(1)}, u32[]{:S(2)}, u32[]{:S(2)}) collective-permute-start(f32[4,12,9216]{2,0,1:T(4,128)S(1)} %get-tuple-element.101), channel_id=1, source_target_pairs={{24,0},{0,8},{8,16},{16,24},{25,1},{1,9},{9,17},{17,25},{26,2},{2,... | collective-permute-start | bytes 5308424 | tf_op jit(solution)/shard_map/while/body/ppermute | solution.py:20
  49.8 41.6 %collective-permute-start = (f32[4,12,9216]{2,0,1:T(4,128)S(1)}, f32[4,12,9216]{2,0,1:T(4,128)S(1)}, u32[]{:S(2)}, u32[]{:S(2)}) collective-permute-start(f32[4,12,9216]{2,0,1:T(4,128)S(1)} %get-tuple-element.101), channel_id=1, source_target_pairs={{24,0},{0,8},{8,16},{16,24},{25,1},{1,9},{9,17},{17,25},{26,2},{2,... | collective-permute-start | bytes 5308424 | tf_op jit(solution)/shard_map/while/body/ppermute | solution.py:20
  92.2 40.7 %collective-permute-start = (f32[4,12,9216]{2,0,1:T(4,128)S(1)}, f32[4,12,9216]{2,0,1:T(4,128)S(1)}, u32[]{:S(2)}, u32[]{:S(2)}) collective-permute-start(f32[4,12,9216]{2,0,1:T(4,128)S(1)} %get-tuple-element.101), channel_id=1, source_target_pairs={{24,0},{0,8},{8,16},{16,24},{25,1},{1,9},{9,17},{17,25},{26,2},{2,... | collective-permute-start | bytes 5308424 | tf_op jit(solution)/shard_map/while/body/ppermute | solution.py:20
  134.8 1.5 copy-start
  367.7 85.0 %all-to-all-start = ((f32[8,1,221184]{2,1,0:T(1,128)}), f32[8,1,221184]{2,1,0:T(1,128)}, u32[]{:S(2)}, u32[]{:S(2)}) async-start(f32[8,1,221184]{2,1,0:T(1,128)} %reshape.120), calls=%async_computation | async-start | bytes 14155776 | tf_op jit(solution)/shard_map/while/body/eval_jaxpr/all_to_all | solution.py:83
  714.3 5.1 copy-start.4
  714.3 85.2 %all-to-all-start.1 = ((f32[16,96,1152]{2,0,1:T(8,128)}), f32[16,96,1152]{2,0,1:T(8,128)}, u32[]{:S(2)}, u32[]{:S(2)}) async-start(f32[16,96,1152]{2,0,1:T(8,128)} %copy.27), calls=%async_computation.1 | async-start | bytes 14155776 | tf_op jit(solution)/shard_map/while/body/eval_jaxpr/all_to_all | solution.py:69
  879.8 15.9 %copy-start.1 = (f32[4,12,9216]{2,0,1:T(4,128)S(1)}, f32[4,12,9216]{2,0,1:T(4,128)}, u32[]{:S(2)}) copy-start(f32[4,12,9216]{2,0,1:T(4,128)} %param.5) | copy-start | bytes 5308420
  895.8 20.4 %copy-start.3 = (f32[4,12,9216]{2,0,1:T(4,128)}, f32[4,12,9216]{2,0,1:T(4,128)S(1)}, u32[]{:S(2)}) copy-start(f32[4,12,9216]{2,0,1:T(4,128)S(1)} %bitcast_negate_fusion) | copy-start | bytes 5308420
where the time goes:
time: 902 us; the launch traced here: 916 us
  local copies, waits for them, and re-layouts  407 us (45%)
  waiting for transfers between devices  282 us (31%)
  matrix products  109 us (12%)
  other arithmetic  89.3 us (10%)
  starting transfers between devices  13.3 us (1%)
  blocking collectives  11.8 us (1%)
    unnamed x14, local copies, waits for them, and re-layouts  238 us
    ppermute x3, waiting for transfers between devices, passed_along(): return lax.ppermute(block, axis, route)  123 us
    all_to_all x1, waiting for transfers between devices, solve_items(): lax.all_to_all(along, 'grid', split_axis=1, concat_axis=2, tiled=True)  80 us
    all_to_all x1, waiting for transfers between devices, one_group(): lax.all_to_all(spectra, 'grid', split_axis=2, concat_axis=1, tiled=True)  79.4 us
    all_to_all x1, other arithmetic, one_group(): lax.all_to_all(spectra, 'grid', split_axis=2, concat_axis=1, tiled=True)  76.3 us
    reshape x2, local copies, waits for them, and re-layouts, across_planes(): return shaped.reshape(count, planes, NY * NZ)  62.2 us
    dot_general x2, matrix products, across_planes(): shaped = jnp.matmul(shaped, table_z, precision=highest)  47.3 us
    all_to_all x2, local copies, waits for them, and re-layouts, one_group(): lax.all_to_all(spectra, 'grid', split_axis=2, concat_axis=1, tiled=True)  44.8 us
  transfers between devices with their start and end apart: 5, of which 5 were waited for; matrix products, arithmetic and copies ran while one was open for 0% of the time, Pallas kernels for 0%

commit v1 on v0

--- a/solution.py
+++ b/solution.py
@@ -1,13 +1,19 @@
+import functools
 import math
 
 import jax
 import jax.numpy as jnp
+import ml_dtypes
+import numpy as np
 from jax import lax
+from jax.experimental import pallas as pl
+from jax.experimental.pallas import tpu as pltpu
 from jax.sharding import PartitionSpec as P
 
 NX = 96
 NY = 96
 NZ = 96
+LANES = 128
 
 
 box_length = 16.0
@@ -41,7 +47,7 @@
     return shaped.reshape(count, planes, NY * NZ)
 
 
-def shards(orbitals, pair_mask, cycle_step):
+def slab_plan(orbitals, pair_mask, cycle_step):
     orbit_count = orbitals.shape[0]
     planes = orbitals.shape[1]
     grid_count = lax.axis_size("grid")
@@ -97,6 +103,376 @@
     return (exchange_field, projection)
 
 
+SLABS = 8
+GROUP = 4
+SLAB_PLANES = NX // SLABS
+COLS = NY * NZ // LANES
+SLAB_ROWS = SLAB_PLANES * COLS
+QUADS = NY // 4
+
+bf16 = jnp.bfloat16
+f32 = jnp.float32
+in_vmem = pl.BlockSpec(memory_space=pltpu.VMEM)
+in_smem = pl.BlockSpec(memory_space=pltpu.SMEM)
+anywhere = pl.BlockSpec(memory_space=pl.ANY)
+
+
+def high_low(table):
+    high = table.astype(ml_dtypes.bfloat16)
+    return high, (table - high.astype(np.float64)).astype(ml_dtypes.bfloat16)
+
+
+def cas_table(length):
+    index = np.arange(length)
+    angle = (index[:, None] * index[None, :] % length) * (2.0 * np.pi / length)
+    return np.cos(angle) + np.sin(angle)
+
+
+def lane_table(table):
+    high, low = high_low(table)
+    out = np.zeros((2 * LANES, 2 * LANES), high.dtype)
+    for row in (0, LANES):
+        out[row : row + NZ, :NZ] = high
+        out[row : row + NZ, LANES : LANES + NZ] = low
+    return out
+
+
+def row_table(table):
+    high, low = high_low(table)
+    return np.concatenate([np.concatenate([high, high], 1), np.concatenate([low, low], 1)], 0)
+
+
+def plane_order(device):
+    return np.concatenate([np.arange(SLAB_PLANES) + SLAB_PLANES * (device ^ k) for k in range(SLABS)])
+
+
+def coulomb_table():
+    index = np.arange(NY)
+    freq = np.where(index * 2 >= NY, index - NY, index).astype(np.float64) ** 2
+    half = np.arange(NX // 2 + 1, dtype=np.float64) ** 2
+    squares = half[:, None, None] + freq[None, :, None] + freq[None, None, :]
+    scale = box_length * box_length / math.pi / (NX * NY * NZ)
+    out = np.zeros((NX // 2 + 1, NY, LANES), np.float32)
+    out[:, :, :NZ] = np.where(squares > 0.5, scale / np.maximum(squares, 1.0), 0.0)
+    return out
+
+
+def split(value):
+    high = value.astype(bf16)
+    return high, (value - high.astype(f32)).astype(bf16)
+
+
+def product(left, right):
+    return lax.dot_general(left, right, (((1,), (0,)), ((), ())), preferred_element_type=f32)
+
+
+def along_lanes(value, table):
+    both = product(jnp.concatenate(split(value), axis=1), table)
+    return both[:, :LANES] + both[:, LANES:]
+
+
+def along_rows(table, value):
+    both = product(table, jnp.concatenate(split(value), axis=0))
+    half = both.shape[0] // 2
+    return both[:half] + both[half:]
+
+
+def prepare_kernel(place, block, *refs):
+    outs, natural = refs[:-1], refs[-1]
+    me = place[0]
+
+    def two_columns(step, carry):
+        for a in range(GROUP):
+            pair = [block[:, a, pl.ds(pl.multiple_of((2 * step + i) * LANES, LANES), LANES)] for i in range(2)]
+            natural[a, pl.ds(pl.multiple_of(2 * SLAB_PLANES * step, 8), 2 * SLAB_PLANES), :] = jnp.concatenate(pair, 0)
+        return carry
+
+    lax.fori_loop(0, COLS // 2, two_columns, 0, unroll=2)
+    for k in range(GROUP):
+        outs[k][...] = natural[(me & 3) ^ k]
+        outs[GROUP + k][...] = natural[((me >> 2) * 2) ^ k]
+
+
+def prepare(place, block):
+    slab = jax.ShapeDtypeStruct((SLAB_ROWS, LANES), f32)
+    return pl.pallas_call(
+        prepare_kernel,
+        out_shape=[slab] * 8,
+        in_specs=[in_smem, in_vmem],
+        out_specs=[in_vmem] * 8,
+        scratch_shapes=[pltpu.VMEM((GROUP, SLAB_ROWS, LANES), f32)],
+        compiler_params=pltpu.CompilerParams(vmem_limit_bytes=32 << 20),
+        cost_estimate=pl.CostEstimate(flops=0, bytes_accessed=6 << 20, transcendentals=0),
+    )(place, block)
+
+
+def pair_kernel(turn, place, mask, *refs):
+    own_slabs, refs = refs[:SLABS], refs[SLABS:]
+    vis_slabs, refs = refs[:SLABS], refs[SLABS:]
+    table_z, table_y, table_x, table_back, coulomb_hbm, *refs = refs
+    if turn:
+        before_hbm, *refs = refs
+        outs, refs = refs[:SLABS], refs[SLABS:]
+    else:
+        out_hbm, *refs = refs
+    raw, own, vis, spectrum, coulomb, total, in_sems, side_sems, out_sems = refs
+    parts = in_sems.shape[0]
+    part_rows = SLAB_ROWS // parts
+    part_quads = QUADS // parts
+
+    def arrivals(part):
+        rows = pl.ds(part * part_rows, part_rows)
+        return [
+            pltpu.make_async_copy(slab.at[rows], raw.at[i, rows], in_sems.at[part])
+            for i, slab in enumerate((*own_slabs, *vis_slabs))
+        ]
+
+    for part in range(parts):
+        for copy in arrivals(part):
+            copy.start()
+    side = [pltpu.make_async_copy(coulomb_hbm, coulomb, side_sems.at[0])]
+    if turn:
+        side.append(pltpu.make_async_copy(before_hbm, total, side_sems.at[1]))
+    for copy in side:
+        copy.start()
+
+    def in_order(step, first, out):
+        rows = pl.ds(pl.multiple_of(2 * SLAB_PLANES * step, 8), 2 * SLAB_PLANES)
+        pieces = [raw[first + k, rows, :] for k in range(SLABS)]
+        out[2 * step] = jnp.concatenate([piece[:SLAB_PLANES] for piece in pieces], axis=0)
+        out[2 * step + 1] = jnp.concatenate([piece[SLAB_PLANES:] for piece in pieces], axis=0)
+
+    def lane_index():
+        return lax.broadcasted_iota(jnp.int32, (NX, LANES), 1)
+
+    def forward(quad, carry):
+        lane = lane_index()
+        first, second, third = [own[3 * quad + i] * vis[3 * quad + i] for i in range(3)]
+        rows = [
+            first,
+            pltpu.roll(jnp.where(lane >= 96, first, second), 32, 1),
+            pltpu.roll(jnp.where(lane >= 64, second, third), 64, 1),
+            pltpu.roll(third, 96, 1),
+        ]
+        done = along_lanes(jnp.concatenate(rows, axis=0), table_z[...])
+        for j in range(2):
+            both = jnp.concatenate([done[2 * j * NX : (2 * j + 1) * NX], done[(2 * j + 1) * NX : (2 * j + 2) * NX]], 1)
+            both = along_rows(table_x[...], both)
+            spectrum[4 * quad + 2 * j] = both[:, :LANES]
+            spectrum[4 * quad + 2 * j + 1] = both[:, LANES:]
+        return carry
+
+    for part in range(parts):
+        for copy in arrivals(part):
+            copy.wait()
+
+        def relay(step, carry):
+            in_order(step, 0, own)
+            in_order(step, SLABS, vis)
+            return carry
+
+        lax.fori_loop(part * part_quads * 3 // 2, (part + 1) * part_quads * 3 // 2, relay, 0)
+        lax.fori_loop(part * part_quads, (part + 1) * part_quads, forward, 0, unroll=min(4, part_quads))
+    for copy in side:
+        copy.wait()
+
+    def middle(step, carry):
+        base = pl.multiple_of(8 * step, 8)
+        block = jnp.swapaxes(spectrum[:, pl.ds(base, 8), :], 0, 1)
+        rows = []
+        for j in range(4):
+            both = along_rows(table_y[...], jnp.concatenate([block[2 * j], block[2 * j + 1]], axis=1))
+            at = [base + 2 * j, base + 2 * j + 1]
+            both = both * jnp.concatenate([coulomb[jnp.minimum(i, NX - i)] for i in at], axis=1)
+            both = along_rows(table_y[...], both)
+            rows += [both[:, :LANES], both[:, LANES:]]
+        spectrum[:, pl.ds(base, 8), :] = jnp.swapaxes(jnp.stack(rows, axis=0), 0, 1)
+        return carry
+
+    lax.fori_loop(0, NX // 8, middle, 0, unroll=2)
+    me = place[0]
+    weight = -mask[me & 3, (me >> 2) * 2 + turn].astype(f32)
+
+    def back(quad, carry):
+        lane = lane_index()
+        rows = []
+        for j in range(2):
+            both = jnp.concatenate([spectrum[4 * quad + 2 * j], spectrum[4 * quad + 2 * j + 1]], axis=1)
+            both = along_rows(table_back[...], both)
+            rows += [both[:, :LANES], both[:, LANES:]]
+        done = along_lanes(jnp.concatenate(rows, axis=0), table_z[...])
+        first, second, third, fourth = [done[NX * i : NX * (i + 1)] for i in range(4)]
+        second = pltpu.roll(second, 96, 1)
+        third = pltpu.roll(third, 64, 1)
+        fourth = pltpu.roll(fourth, 32, 1)
+        columns = (
+            jnp.where(lane < 96, first, second),
+            jnp.where(lane < 64, second, third),
+            jnp.where(lane < 32, third, fourth),
+        )
+        for i in range(3):
+            value = weight * (columns[i] * vis[3 * quad + i])
+            if turn:
+                value = total[3 * quad + i] + value
+            total[3 * quad + i] = value
+        return carry
+
+    leaving = []
+    for part in range(parts):
+        lax.fori_loop(part * part_quads, (part + 1) * part_quads, back, 0, unroll=min(4, part_quads))
+        if turn:
+
+            def apart(step, carry):
+                rows = pl.ds(pl.multiple_of(2 * SLAB_PLANES * step, 8), 2 * SLAB_PLANES)
+                even, odd = total[2 * step], total[2 * step + 1]
+                for k in range(SLABS):
+                    cut = slice(SLAB_PLANES * k, SLAB_PLANES * (k + 1))
+                    raw[k, rows, :] = jnp.concatenate([even[cut], odd[cut]], axis=0)
+                return carry
+
+            lax.fori_loop(part * part_quads * 3 // 2, (part + 1) * part_quads * 3 // 2, apart, 0)
+            rows = pl.ds(part * part_rows, part_rows)
+            copies = [pltpu.make_async_copy(raw.at[k, rows], outs[k].at[rows], out_sems.at[part]) for k in range(SLABS)]
+        else:
+            cols = pl.ds(part * part_quads * 3, part_quads * 3)
+            copies = [pltpu.make_async_copy(total.at[cols], out_hbm.at[cols], out_sems.at[part])]
+        for copy in copies:
+            copy.start()
+        leaving += copies
+    for copy in leaving:
+        copy.wait()
+
+
+def pair_step(turn, place, mask, own_slabs, vis_slabs, tables, before=None):
+    parts = 4
+    extra = [] if before is None else [before]
+    whole = jax.ShapeDtypeStruct((COLS, NX, LANES), f32)
+    slab = jax.ShapeDtypeStruct((SLAB_ROWS, LANES), f32)
+    return pl.pallas_call(
+        functools.partial(pair_kernel, turn),
+        out_shape=[slab] * SLABS if turn else whole,
+        in_specs=[in_smem] * 2 + [anywhere] * (2 * SLABS) + [in_vmem] * 4 + [anywhere] * (1 + len(extra)),
+        out_specs=[anywhere] * SLABS if turn else anywhere,
+        scratch_shapes=[
+            pltpu.VMEM((2 * SLABS, SLAB_ROWS, LANES), f32),
+            pltpu.VMEM((COLS, NX, LANES), f32),
+            pltpu.VMEM((COLS, NX, LANES), f32),
+            pltpu.VMEM((NY, NX, LANES), f32),
+            pltpu.VMEM((NX // 2 + 1, NY, LANES), f32),
+            pltpu.VMEM((COLS, NX, LANES), f32),
+            pltpu.SemaphoreType.DMA((parts,)),
+            pltpu.SemaphoreType.DMA((2,)),
+            pltpu.SemaphoreType.DMA((parts,)),
+        ],
+        compiler_params=pltpu.CompilerParams(vmem_limit_bytes=40 << 20),
+        cost_estimate=pl.CostEstimate(flops=16 * 10**9, bytes_accessed=16 << 20, transcendentals=0),
+    )(place, mask, *own_slabs, *vis_slabs, *tables, *extra)
+
+
+def finish_kernel(place, *refs):
+    parts, refs = refs[:SLABS], refs[SLABS:]
+    own, refs = refs[:GROUP], refs[GROUP:]
+    out, gram, natural = refs
+    me = place[0] & 3
+    for k in range(GROUP):
+        natural[me ^ k] = parts[k][...] + parts[k + GROUP][...]
+    sums = []
+    for a in range(GROUP):
+        for c in range(GROUP):
+            terms = own[a][...] * natural[me ^ c]
+            terms = jnp.sum(terms.reshape(SLAB_ROWS // 8, 8, LANES), axis=0)
+            sums.append(jnp.sum(terms, axis=0, keepdims=True))
+    gram[...] = jnp.concatenate(sums, axis=0)
+
+    def two_columns(step, carry):
+        rows = pl.ds(pl.multiple_of(2 * SLAB_PLANES * step, 8), 2 * SLAB_PLANES)
+        for a in range(GROUP):
+            pair = natural[a, rows, :]
+            for i in range(2):
+                lanes = pl.ds(pl.multiple_of((2 * step + i) * LANES, LANES), LANES)
+                out[:, a, lanes] = pair[SLAB_PLANES * i : SLAB_PLANES * (i + 1)]
+        return carry
+
+    lax.fori_loop(0, COLS // 2, two_columns, 0, unroll=2)
+
+
+def finish(place, parts, own):
+    return pl.pallas_call(
+        finish_kernel,
+        out_shape=[
+            jax.ShapeDtypeStruct((SLAB_PLANES, GROUP, NY * NZ), f32),
+            jax.ShapeDtypeStruct((GROUP * GROUP, LANES), f32),
+        ],
+        in_specs=[in_smem] + [in_vmem] * (SLABS + GROUP),
+        out_specs=[in_vmem] * 2,
+        scratch_shapes=[pltpu.VMEM((GROUP, SLAB_ROWS, LANES), f32)],
+        compiler_params=pltpu.CompilerParams(vmem_limit_bytes=32 << 20),
+        cost_estimate=pl.CostEstimate(flops=0, bytes_accessed=8 << 20, transcendentals=0),
+    )(place, *parts, *own)
+
+
+def to_partner(block, flip):
+    return lax.ppermute(block, "grid", [(i, i ^ flip) for i in range(SLABS)])
+
+
+def to_group(block, distance, flip):
+    bands = lax.axis_size("band")
+    route = [(b * SLABS + i, (b + distance) % bands * SLABS + (i ^ flip)) for b in range(bands) for i in range(SLABS)]
+    return lax.ppermute(block, ("band", "grid"), route)
+
+
+def pair_plan(orbitals, pair_mask, cycle_step):
+    me = lax.axis_index("grid")
+    place = me.astype(jnp.int32).reshape(1)
+    cas = cas_table(NX)
+    forward_x = np.stack([row_table(cas[:, plane_order(d)]) for d in range(SLABS)])
+    back_x = np.stack([row_table(cas[plane_order(d), :]) for d in range(SLABS)])
+    tables = (
+        jnp.asarray(lane_table(cas)),
+        jnp.asarray(row_table(cas)),
+        lax.dynamic_index_in_dim(jnp.asarray(forward_x), me, keepdims=False),
+        lax.dynamic_index_in_dim(jnp.asarray(back_x), me, keepdims=False),
+        jnp.asarray(coulomb_table()),
+    )
+    slabs = prepare(place, jnp.transpose(orbitals, (1, 0, 2)))
+
+    def with_distance(distance, slabs, pair_mask, place, tables):
+        own_out, vis_out = slabs[:GROUP], slabs[GROUP:]
+        vis = [[to_group(vis_out[t], distance, 0), to_group(vis_out[2 + t], distance, 4)] for t in range(2)]
+        own = [own_out[0]] + [to_partner(own_out[k], k) for k in range(1, GROUP)]
+        own += [to_partner(own[k], 4) for k in range(GROUP)]
+        visiting = []
+        for t in range(2):
+            home, across = vis[t]
+            beside, diagonal = to_partner(home, 2), to_partner(across, 2)
+            cored = [to_partner(slab, 1) for slab in (home, beside, across, diagonal)]
+            visiting.append([home, cored[0], beside, cored[1], across, cored[2], diagonal, cored[3]])
+        total = pair_step(0, place, pair_mask, own, visiting[0], tables)
+        parts = pair_step(1, place, pair_mask, own, visiting[1], tables, total)
+        parts = [parts[0]] + [to_partner(parts[k], k) for k in range(1, SLABS)]
+        return finish(place, parts, own_out)
+
+    bands = lax.axis_size("band")
+    field, gram = lax.switch(
+        cycle_step - 1,
+        [functools.partial(with_distance, distance) for distance in range(1, bands)],
+        slabs,
+        pair_mask,
+        place,
+        tables,
+    )
+    gram = jnp.sum(gram, axis=1).reshape(GROUP, GROUP) / (NX * NY * NZ)
+    order = (me & 3) ^ jnp.arange(GROUP, dtype=jnp.int32)
+    gram = jnp.take(jnp.take(gram, order, axis=0), order, axis=1)
+    return jnp.transpose(field, (1, 0, 2)), lax.psum(gram, "grid")
+
+
+def shards(orbitals, pair_mask, cycle_step):
+    if lax.axis_size("grid") == SLABS and orbitals.shape[0] == GROUP:
+        return pair_plan(orbitals, pair_mask, cycle_step)
+    return slab_plan(orbitals, pair_mask, cycle_step)
+
+
 def solution(mesh):
     return jax.shard_map(
         shards,

time: 902 us -> 235 us (0.26); the launches traced: 916 us -> 233 us
  local copies, waits for them, and re-layouts: 407 us -> 4.4 us
  waiting for transfers between devices: 282 us -> 100 us
  matrix products: 109 us -> 0 us
  other arithmetic: 89.3 us -> 0.29 us
  Pallas kernels: 0 us -> 76 us
  starting transfers between devices: 13.3 us -> 29.4 us
    unnamed x14 -> x5, local copies, waits for them, and re-layouts: 238 us -> 2.14 us
    all_to_all x2 -> x0, waiting for transfers between devices: 159 us -> none  [the longest x1 80 us: solve_items(): lax.all_to_all(along, 'grid', split_axis=1, concat_axis=2, tiled=True)]
    dot_general x8 -> x0, matrix products: 109 us -> none  [the longest x2 47.3 us: across_planes(): shaped = jnp.matmul(shaped, table_z, precision=highest)]
    all_to_all x1 -> x0, other arithmetic: 76.3 us -> none  [one_group(): lax.all_to_all(spectra, 'grid', split_axis=2, concat_axis=1, tiled=True)]
    pallas_call x0 -> x4, Pallas kernels: none -> 76 us  [the longest x2 70.2 us: pair_step(): pl.pallas_call(functools.partial(pair_kernel, turn), out_shape=[slab] * S...]
    reshape x3 -> x1, local copies, waits for them, and re-layouts: 73.6 us -> 0.08 us  [pair_plan(): gram = jnp.sum(gram, axis=1).reshape(GROUP, GROUP) / (NX * NY * NZ)]
    all_to_all x3 -> x0, local copies, waits for them, and re-layouts: 54.8 us -> none  [the longest x2 44.8 us: one_group(): lax.all_to_all(spectra, 'grid', split_axis=2, concat_axis=1, tiled=True)]
    ppermute x3 -> x30, starting transfers between devices: 3.19 us -> 29.4 us  [the longest x26 21.7 us: to_partner(): return lax.ppermute(block, 'grid', [(i, i ^ flip) for i in range(SLABS)])]
  transfers between devices with their start and end apart: 5 -> 30, of which waited for: 5 -> 12; matrix products, arithmetic and copies ran while one was open for 0% -> 0% of each run, Pallas kernels for 0% -> 14%
where the time goes in v1:
time: 235 us; the launch traced here: 233 us
  waiting for transfers between devices  100 us (43%)
  Pallas kernels  76 us (32%)
  starting transfers between devices  29.4 us (13%)
  blocking collectives  14 us (6%)
  loops' own time  6.95 us (3%)
  local copies, waits for them, and re-layouts  4.4 us (2%)
    ppermute x26, waiting for transfers between devices, to_partner(): return lax.ppermute(block, 'grid', [(i, i ^ flip) for i in range(SLABS)])  83.7 us
    pallas_call x2, Pallas kernels, pair_step(): pl.pallas_call(functools.partial(pair_kernel, turn), out_shape=[slab] * S...  70.2 us
    ppermute x26, starting transfers between devices, to_partner(): return lax.ppermute(block, 'grid', [(i, i ^ flip) for i in range(SLABS)])  21.7 us
    ppermute x4, waiting for transfers between devices, to_group(): return lax.ppermute(block, ('band', 'grid'), route)  16.4 us
    psum x1, blocking collectives, pair_plan(): return (jnp.transpose(field, (1, 0, 2)), lax.psum(gram, 'grid'))  14 us
    ppermute x4, starting transfers between devices, to_group(): return lax.ppermute(block, ('band', 'grid'), route)  7.74 us
    another operation x1, loops' own time, pair_plan(): lax.switch(cycle_step - 1, [functools.partial(with_distance, distance) fo...  6.95 us
  transfers between devices with their start and end apart: 30, of which 12 were waited for; matrix products, arithmetic and copies ran while one was open for 0% of the time, Pallas kernels for 14%

profile of v1, /device:TPU:0, one launch (start us, length us, event | category | flops | bytes accessed | tf_op | source)
XLA Modules:
  0.0 232.8 jit_solution(2838627113677162902)
XLA Ops:
  0.7 1.5 copy-done
  2.1 1.5 shard_map.95
  4.3 212.2 %conditional.1 = (f32[12,4,9216]{2,1,0:T(4,128)}, f32[4,4]{1,0:T(4,128)S(1)}) conditional(s32[]{:T(128)} %clamp.3, (f32[864,128]{1,0:T(8,128)S(1)}, f32[864,128]{1,0:T(8,128)S(1)}, f32[864,128]{1,0:T(8,128)S(1)}, f32[864,128]{1,0:T(8,128)S(1)}, f32[864,128]{1,0:T(8,128)S(1)}, /*index=5*/f32[864,128]{1,0:T(8,128)S(1)}, ...), branch_computations={%region_0.0_spmd, %region_2.0_spmd, %region_4.6_spmd} | conditional | flops 32000002048 | bytes 105784800 | solution.py:456
  4.3 0.5 collective-permute-start
  4.8 2.6 %collective-permute-start.1 = (f32[864,128]{1,0:T(8,128)S(1)}, f32[864,128]{1,0:T(8,128)S(1)}, u32[]{:S(2)}, u32[]{:S(2)}) collective-permute-start(f32[864,128]{1,0:T(8,128)S(1)} %get-tuple-element.128.refs_10_), channel_id=1, source_target_pairs={{0,2},{1,3},{2,0},{3,1},{4,6},{5,7},{6,4},{7,5},{8,10},{9,11},{10,... | collective-permute-start | bytes 1327112 | tf_op jit(solution)/shard_map/cond/branch_0_fun/ppermute | solution.py:415
  7.4 1.8 collective-permute-start.3
  9.2 1.6 collective-permute-start.15
  10.8 1.5 collective-permute-start.19
  12.3 6.1 %collective-permute-done.1.refs_2_ = f32[864,128]{1,0:T(8,128)S(1)} collective-permute-done((f32[864,128]{1,0:T(8,128)S(1)}, f32[864,128]{1,0:T(8,128)S(1)}, u32[]{:S(2)}, u32[]{:S(2)}) %collective-permute-start.1) | collective-permute-done | bytes 442400 | tf_op jit(solution)/shard_map/cond/branch_0_fun/ppermute | solution.py:415
  18.4 2.0 collective-permute-start.7
  20.4 6.9 %collective-permute-done.2.refs_3_ = f32[864,128]{1,0:T(8,128)S(1)} collective-permute-done((f32[864,128]{1,0:T(8,128)S(1)}, f32[864,128]{1,0:T(8,128)S(1)}, u32[]{:S(2)}, u32[]{:S(2)}) %collective-permute-start.2) | collective-permute-done | bytes 442400 | tf_op jit(solution)/shard_map/cond/branch_0_fun/ppermute | solution.py:415
  27.4 2.6 %collective-permute-start.11 = (f32[864,128]{1,0:T(8,128)S(1)}, f32[864,128]{1,0:T(8,128)S(1)}, u32[]{:S(2)}, u32[]{:S(2)}) collective-permute-start(f32[864,128]{1,0:T(8,128)S(1)} %get-tuple-element.131), channel_id=1, source_target_pairs={{0,12},{1,13},{2,14},{3,15},{4,8},{5,9},{6,10},{7,11},{8,20},{9,21... | collective-permute-start | bytes 1327112 | tf_op jit(solution)/shard_map/cond/branch_0_fun/ppermute | solution.py:421
  30.0 0.5 collective-permute-start.4
  30.5 1.5 collective-permute-start.5
  32.0 1.2 collective-permute-done.19.refs_12_
  33.2 1.8 collective-permute-start.6
  35.0 8.0 %collective-permute-done.7.refs_8_ = f32[864,128]{1,0:T(8,128)S(1)} collective-permute-done((f32[864,128]{1,0:T(8,128)S(1)}, f32[864,128]{1,0:T(8,128)S(1)}, u32[]{:S(2)}, u32[]{:S(2)}) %collective-permute-start.7) | collective-permute-done | bytes 442400 | tf_op jit(solution)/shard_map/cond/branch_0_fun/ppermute | solution.py:421
  43.0 1.5 collective-permute-start.17
  44.5 7.2 %collective-permute-done.11.refs_12_ = f32[864,128]{1,0:T(8,128)S(1)} collective-permute-done((f32[864,128]{1,0:T(8,128)S(1)}, f32[864,128]{1,0:T(8,128)S(1)}, u32[]{:S(2)}, u32[]{:S(2)}) %collective-permute-start.11) | collective-permute-done | bytes 442400 | tf_op jit(solution)/shard_map/cond/branch_0_fun/ppermute | solution.py:421
  51.7 1.5 collective-permute-start.21
  53.2 8.7 %collective-permute-done.5.refs_6_ = f32[864,128]{1,0:T(8,128)S(1)} collective-permute-done((f32[864,128]{1,0:T(8,128)S(1)}, f32[864,128]{1,0:T(8,128)S(1)}, u32[]{:S(2)}, u32[]{:S(2)}) %collective-permute-start.5) | collective-permute-done | bytes 442400 | tf_op jit(solution)/shard_map/cond/branch_0_fun/ppermute | solution.py:415
  61.9 9.0 %collective-permute-done.6.refs_7_ = f32[864,128]{1,0:T(8,128)S(1)} collective-permute-done((f32[864,128]{1,0:T(8,128)S(1)}, f32[864,128]{1,0:T(8,128)S(1)}, u32[]{:S(2)}, u32[]{:S(2)}) %collective-permute-start.6) | collective-permute-done | bytes 442400 | tf_op jit(solution)/shard_map/cond/branch_0_fun/ppermute | solution.py:415
  70.9 1.6 collective-permute-start.9
  72.6 0.4 collective-permute-start.13
  73.0 0.5 collective-permute-start.22
  73.5 1.0 dynamic-slice_bitcast_fusion
  74.5 0.1 collective-permute-start.12
  74.6 9.4 %collective-permute-done.9.refs_10_ = f32[864,128]{1,0:T(8,128)S(1)} collective-permute-done((f32[864,128]{1,0:T(8,128)S(1)}, f32[864,128]{1,0:T(8,128)S(1)}, u32[]{:S(2)}, u32[]{:S(2)}) %collective-permute-start.9) | collective-permute-done | bytes 442400 | tf_op jit(solution)/shard_map/cond/branch_0_fun/ppermute | solution.py:415
  84.0 8.1 %collective-permute-done.13.refs_14_ = f32[864,128]{1,0:T(8,128)S(1)} collective-permute-done((f32[864,128]{1,0:T(8,128)S(1)}, f32[864,128]{1,0:T(8,128)S(1)}, u32[]{:S(2)}, u32[]{:S(2)}) %collective-permute-start.13) | collective-permute-done | bytes 442400 | tf_op jit(solution)/shard_map/cond/branch_0_fun/ppermute | solution.py:415
  92.2 0.5 collective-permute-start.14
  92.7 32.6 %branch_0_fun.3.refs_21_ = f32[72,96,128]{2,1,0:T(8,128)S(1)} custom-call(s32[1]{0:T(128)} %get-tuple-element.124.place, s32[4,4]{1,0:T(4,128)S(1)} %get-tuple-element.125.mask, f32[864,128]{1,0:T(8,128)S(1)} %get-tuple-element.126.refs_0_.refs_8_, f32[864,128]{1,0:T(8,128)S(1)} %collective-permute-done.refs_1_, ...), custom_call_target="tpu_custom_call" | custom-call | flops 16000000000 | bytes 16777216 | tf_op jit(solution)/shard_map/cond/branch_0_fun/pallas_call | solution.py:351
  125.4 37.5 %branch_0_fun.4 = (f32[864,128]{1,0:T(8,128)S(1)}, f32[864,128]{1,0:T(8,128)S(1)}, f32[864,128]{1,0:T(8,128)S(1)}, f32[864,128]{1,0:T(8,128)S(1)}, f32[864,128]{...) custom-call(s32[1]{0:T(128)} %get-tuple-element.124.place, ...), custom_call_target="tpu_custom_call" | custom-call | flops 16000000000 | bytes 16777216 | tf_op jit(solution)/shard_map/cond/branch_0_fun/pallas_call | solution.py:351
  162.9 0.1 collective-permute-start.23
  163.0 1.8 collective-permute-start.24
  164.9 1.2 collective-permute-start.26
  166.1 0.4 collective-permute-start.27
  166.6 2.2 collective-permute-start.28
  168.8 7.3 %collective-permute-done.24.refs_2_ = f32[864,128]{1,0:T(8,128)S(1)} collective-permute-done((f32[864,128]{1,0:T(8,128)S(1)}, f32[864,128]{1,0:T(8,128)S(1)}, u32[]{:S(2)}, u32[]{:S(2)}) %collective-permute-start.24) | collective-permute-done | bytes 442400 | tf_op jit(solution)/shard_map/cond/branch_0_fun/ppermute | solution.py:415
  176.0 1.0 collective-permute-start.29
  177.0 7.7 %collective-permute-done.25.refs_3_ = f32[864,128]{1,0:T(8,128)S(1)} collective-permute-done((f32[864,128]{1,0:T(8,128)S(1)}, f32[864,128]{1,0:T(8,128)S(1)}, u32[]{:S(2)}, u32[]{:S(2)}) %collective-permute-start.25) | collective-permute-done | bytes 442400 | tf_op jit(solution)/shard_map/cond/branch_0_fun/ppermute | solution.py:415
  184.8 20.3 %collective-permute-done.27.refs_5_ = f32[864,128]{1,0:T(8,128)S(1)} collective-permute-done((f32[864,128]{1,0:T(8,128)S(1)}, f32[864,128]{1,0:T(8,128)S(1)}, u32[]{:S(2)}, u32[]{:S(2)}) %collective-permute-start.27) | collective-permute-done | bytes 442400 | tf_op jit(solution)/shard_map/cond/branch_0_fun/ppermute | solution.py:415
  205.1 4.3 %branch_0_fun.5 = (f32[12,4,9216]{2,1,0:T(4,128)}, f32[16,128]{1,0:T(8,128)S(1)}) custom-call(s32[1]{0:T(128)} %get-tuple-element.124.place, f32[864,128]{1,0:T(8,128)S(1)} %get-tuple-element.140.refs_0_, f32[864,128]{1,0:T(8,128)S(1)} %collective-permute-done.23.refs_1_, f32[864,128]{1,0:T(8,128)S(1)} %collective-permute-done.24.refs_2_, ...), custom_call_target="tpu_custom_call" | custom-call | bytes 8388608 | tf_op jit(solution)/shard_map/cond/branch_0_fun/pallas_call | solution.py:400
  209.5 0.1 reduce_sum.14
  216.5 0.6 gather_fusion
  217.2 0.1 copy.10
  217.3 0.6 gather_fusion.1
  217.9 14.0 %psum.7 = f32[4,4]{0,1:T(4,128)S(1)} all-reduce(f32[4,4]{0,1:T(4,128)S(1)} %select_bitcast_fusion), channel_id=1, replica_groups=mesh['band'=4,'grid'=8] {'grid'}, use_global_device_ids=true, to_apply=%region_6.7 | all-reduce | flops 16 | bytes 128 | tf_op jit(solution)/shard_map/psum | solution.py:467
  231.9 0.7 copy.11
  (41 shorter events, 0.5 us)
Async XLA Ops:
  0.6 3.6 %copy-start.1 = (s32[4,4]{1,0:T(4,128)S(1)}, s32[4,4]{1,0:T(4,128)}, u32[]{:S(2)}) copy-start(s32[4,4]{1,0:T(4,128)} %param.12) | copy-start | bytes 196
  0.6 1.5 copy-start
  4.3 6.5 %collective-permute-start = (f32[864,128]{1,0:T(8,128)S(1)}, f32[864,128]{1,0:T(8,128)S(1)}, u32[]{:S(2)}, u32[]{:S(2)}) collective-permute-start(f32[864,128]{1,0:T(8,128)S(1)} %get-tuple-element.127.refs_9_), channel_id=1, source_target_pairs={{0,1},{1,0},{2,3},{3,2},{4,5},{5,4},{6,7},{7,6},{8,9},{9,8},{10,11... | collective-permute-start | bytes 1327112 | tf_op jit(solution)/shard_map/cond/branch_0_fun/ppermute | solution.py:415
  4.8 13.6 %collective-permute-start.1 = (f32[864,128]{1,0:T(8,128)S(1)}, f32[864,128]{1,0:T(8,128)S(1)}, u32[]{:S(2)}, u32[]{:S(2)}) collective-permute-start(f32[864,128]{1,0:T(8,128)S(1)} %get-tuple-element.128.refs_10_), channel_id=1, source_target_pairs={{0,2},{1,3},{2,0},{3,1},{4,6},{5,7},{6,4},{7,5},{8,10},{9,11},{10,... | collective-permute-start | bytes 1327112 | tf_op jit(solution)/shard_map/cond/branch_0_fun/ppermute | solution.py:415
  7.4 20.0 %collective-permute-start.2 = (f32[864,128]{1,0:T(8,128)S(1)}, f32[864,128]{1,0:T(8,128)S(1)}, u32[]{:S(2)}, u32[]{:S(2)}) collective-permute-start(f32[864,128]{1,0:T(8,128)S(1)} %get-tuple-element.129.refs_11_), channel_id=1, source_target_pairs={{0,3},{1,2},{2,1},{3,0},{4,7},{5,6},{6,5},{7,4},{8,11},{9,10},{10,... | collective-permute-start | bytes 1327112 | tf_op jit(solution)/shard_map/cond/branch_0_fun/ppermute | solution.py:415
  7.4 22.5 %collective-permute-start.3 = (f32[864,128]{1,0:T(8,128)S(1)}, f32[864,128]{1,0:T(8,128)S(1)}, u32[]{:S(2)}, u32[]{:S(2)}) collective-permute-start(f32[864,128]{1,0:T(8,128)S(1)} %get-tuple-element.126.refs_0_.refs_8_), channel_id=1, source_target_pairs={{0,4},{1,5},{2,6},{3,7},{4,0},{5,1},{6,2},{7,3},{8,12},{9,13},{10,... | collective-permute-start | bytes 1327112 | tf_op jit(solution)/shard_map/cond/branch_0_fun/ppermute | solution.py:415
  9.2 21.3 %collective-permute-start.15 = (f32[864,128]{1,0:T(8,128)S(1)}, f32[864,128]{1,0:T(8,128)S(1)}, u32[]{:S(2)}, u32[]{:S(2)}) collective-permute-start(f32[864,128]{1,0:T(8,128)S(1)} %get-tuple-element.138), channel_id=1, source_target_pairs={{0,8},{1,9},{2,10},{3,11},{4,12},{5,13},{6,14},{7,15},{8,16},{9,17... | collective-permute-start | bytes 1327112 | tf_op jit(solution)/shard_map/cond/branch_0_fun/ppermute | solution.py:421
  10.8 22.4 %collective-permute-start.19 = (f32[864,128]{1,0:T(8,128)S(1)}, f32[864,128]{1,0:T(8,128)S(1)}, u32[]{:S(2)}, u32[]{:S(2)}) collective-permute-start(f32[864,128]{1,0:T(8,128)S(1)} %get-tuple-element.139), channel_id=1, source_target_pairs={{0,12},{1,13},{2,14},{3,15},{4,8},{5,9},{6,10},{7,11},{8,20},{9,21... | collective-permute-start | bytes 1327112 | tf_op jit(solution)/shard_map/cond/branch_0_fun/ppermute | solution.py:421
  18.4 24.6 %collective-permute-start.7 = (f32[864,128]{1,0:T(8,128)S(1)}, f32[864,128]{1,0:T(8,128)S(1)}, u32[]{:S(2)}, u32[]{:S(2)}) collective-permute-start(f32[864,128]{1,0:T(8,128)S(1)} %get-tuple-element.130), channel_id=1, source_target_pairs={{0,8},{1,9},{2,10},{3,11},{4,12},{5,13},{6,14},{7,15},{8,16},{9,17... | collective-permute-start | bytes 1327112 | tf_op jit(solution)/shard_map/cond/branch_0_fun/ppermute | solution.py:421
  27.4 24.3 %collective-permute-start.11 = (f32[864,128]{1,0:T(8,128)S(1)}, f32[864,128]{1,0:T(8,128)S(1)}, u32[]{:S(2)}, u32[]{:S(2)}) collective-permute-start(f32[864,128]{1,0:T(8,128)S(1)} %get-tuple-element.131), channel_id=1, source_target_pairs={{0,12},{1,13},{2,14},{3,15},{4,8},{5,9},{6,10},{7,11},{8,20},{9,21... | collective-permute-start | bytes 1327112 | tf_op jit(solution)/shard_map/cond/branch_0_fun/ppermute | solution.py:421
  30.0 23.2 %collective-permute-start.4 = (f32[864,128]{1,0:T(8,128)S(1)}, f32[864,128]{1,0:T(8,128)S(1)}, u32[]{:S(2)}, u32[]{:S(2)}) collective-permute-start(f32[864,128]{1,0:T(8,128)S(1)} %collective-permute-done.refs_1_), channel_id=1, source_target_pairs={{0,4},{1,5},{2,6},{3,7},{4,0},{5,1},{6,2},{7,3},{8,12},{9,13},{10,... | collective-permute-start | bytes 1327112 | tf_op jit(solution)/shard_map/cond/branch_0_fun/ppermute | solution.py:415
  30.5 31.4 %collective-permute-start.5 = (f32[864,128]{1,0:T(8,128)S(1)}, f32[864,128]{1,0:T(8,128)S(1)}, u32[]{:S(2)}, u32[]{:S(2)}) collective-permute-start(f32[864,128]{1,0:T(8,128)S(1)} %collective-permute-done.1.refs_2_), channel_id=1, source_target_pairs={{0,4},{1,5},{2,6},{3,7},{4,0},{5,1},{6,2},{7,3},{8,12},{9,13},{10,... | collective-permute-start | bytes 1327112 | tf_op jit(solution)/shard_map/cond/branch_0_fun/ppermute | solution.py:415
  33.2 37.7 %collective-permute-start.6 = (f32[864,128]{1,0:T(8,128)S(1)}, f32[864,128]{1,0:T(8,128)S(1)}, u32[]{:S(2)}, u32[]{:S(2)}) collective-permute-start(f32[864,128]{1,0:T(8,128)S(1)} %collective-permute-done.2.refs_3_), channel_id=1, source_target_pairs={{0,4},{1,5},{2,6},{3,7},{4,0},{5,1},{6,2},{7,3},{8,12},{9,13},{10,... | collective-permute-start | bytes 1327112 | tf_op jit(solution)/shard_map/cond/branch_0_fun/ppermute | solution.py:415
  43.0 29.6 %collective-permute-start.17 = (f32[864,128]{1,0:T(8,128)S(1)}, f32[864,128]{1,0:T(8,128)S(1)}, u32[]{:S(2)}, u32[]{:S(2)}) collective-permute-start(f32[864,128]{1,0:T(8,128)S(1)} %collective-permute-done.15.refs_8_), channel_id=1, source_target_pairs={{0,2},{1,3},{2,0},{3,1},{4,6},{5,7},{6,4},{7,5},{8,10},{9,11},{10,... | collective-permute-start | bytes 1327112 | tf_op jit(solution)/shard_map/cond/branch_0_fun/ppermute | solution.py:415
  51.7 21.3 %collective-permute-start.21 = (f32[864,128]{1,0:T(8,128)S(1)}, f32[864,128]{1,0:T(8,128)S(1)}, u32[]{:S(2)}, u32[]{:S(2)}) collective-permute-start(f32[864,128]{1,0:T(8,128)S(1)} %collective-permute-done.19.refs_12_), channel_id=1, source_target_pairs={{0,2},{1,3},{2,0},{3,1},{4,6},{5,7},{6,4},{7,5},{8,10},{9,11},{10,... | collective-permute-start | bytes 1327112 | tf_op jit(solution)/shard_map/cond/branch_0_fun/ppermute | solution.py:415
  53.2 19.8 %collective-permute-start.16 = (f32[864,128]{1,0:T(8,128)S(1)}, f32[864,128]{1,0:T(8,128)S(1)}, u32[]{:S(2)}, u32[]{:S(2)}) collective-permute-start(f32[864,128]{1,0:T(8,128)S(1)} %collective-permute-done.15.refs_8_), channel_id=1, source_target_pairs={{0,1},{1,0},{2,3},{3,2},{4,5},{5,4},{6,7},{7,6},{8,9},{9,8},{10,11... | collective-permute-start | bytes 1327112 | tf_op jit(solution)/shard_map/cond/branch_0_fun/ppermute | solution.py:415
  61.9 12.5 %collective-permute-start.20 = (f32[864,128]{1,0:T(8,128)S(1)}, f32[864,128]{1,0:T(8,128)S(1)}, u32[]{:S(2)}, u32[]{:S(2)}) collective-permute-start(f32[864,128]{1,0:T(8,128)S(1)} %collective-permute-done.19.refs_12_), channel_id=1, source_target_pairs={{0,1},{1,0},{2,3},{3,2},{4,5},{5,4},{6,7},{7,6},{8,9},{9,8},{10,11... | collective-permute-start | bytes 1327112 | tf_op jit(solution)/shard_map/cond/branch_0_fun/ppermute | solution.py:415
  70.9 13.1 %collective-permute-start.9 = (f32[864,128]{1,0:T(8,128)S(1)}, f32[864,128]{1,0:T(8,128)S(1)}, u32[]{:S(2)}, u32[]{:S(2)}) collective-permute-start(f32[864,128]{1,0:T(8,128)S(1)} %collective-permute-done.7.refs_8_), channel_id=1, source_target_pairs={{0,2},{1,3},{2,0},{3,1},{4,6},{5,7},{6,4},{7,5},{8,10},{9,11},{10,... | collective-permute-start | bytes 1327112 | tf_op jit(solution)/shard_map/cond/branch_0_fun/ppermute | solution.py:415
  72.6 19.6 %collective-permute-start.13 = (f32[864,128]{1,0:T(8,128)S(1)}, f32[864,128]{1,0:T(8,128)S(1)}, u32[]{:S(2)}, u32[]{:S(2)}) collective-permute-start(f32[864,128]{1,0:T(8,128)S(1)} %collective-permute-done.11.refs_12_), channel_id=1, source_target_pairs={{0,2},{1,3},{2,0},{3,1},{4,6},{5,7},{6,4},{7,5},{8,10},{9,11},{10,... | collective-permute-start | bytes 1327112 | tf_op jit(solution)/shard_map/cond/branch_0_fun/ppermute | solution.py:415
  73.0 19.2 %collective-permute-start.18 = (f32[864,128]{1,0:T(8,128)S(1)}, f32[864,128]{1,0:T(8,128)S(1)}, u32[]{:S(2)}, u32[]{:S(2)}) collective-permute-start(f32[864,128]{1,0:T(8,128)S(1)} %collective-permute-done.17.refs_10_), channel_id=1, source_target_pairs={{0,1},{1,0},{2,3},{3,2},{4,5},{5,4},{6,7},{7,6},{8,9},{9,8},{10,11... | collective-permute-start | bytes 1327112 | tf_op jit(solution)/shard_map/cond/branch_0_fun/ppermute | solution.py:415
  73.0 19.7 %collective-permute-start.22 = (f32[864,128]{1,0:T(8,128)S(1)}, f32[864,128]{1,0:T(8,128)S(1)}, u32[]{:S(2)}, u32[]{:S(2)}) collective-permute-start(f32[864,128]{1,0:T(8,128)S(1)} %collective-permute-done.21.refs_14_), channel_id=1, source_target_pairs={{0,1},{1,0},{2,3},{3,2},{4,5},{5,4},{6,7},{7,6},{8,9},{9,8},{10,11... | collective-permute-start | bytes 1327112 | tf_op jit(solution)/shard_map/cond/branch_0_fun/ppermute | solution.py:415
  74.5 50.9 %collective-permute-start.12 = (f32[864,128]{1,0:T(8,128)S(1)}, f32[864,128]{1,0:T(8,128)S(1)}, u32[]{:S(2)}, u32[]{:S(2)}) collective-permute-start(f32[864,128]{1,0:T(8,128)S(1)} %collective-permute-done.11.refs_12_), channel_id=1, source_target_pairs={{0,1},{1,0},{2,3},{3,2},{4,5},{5,4},{6,7},{7,6},{8,9},{9,8},{10,11... | collective-permute-start | bytes 1327112 | tf_op jit(solution)/shard_map/cond/branch_0_fun/ppermute | solution.py:415
  84.0 41.3 %collective-permute-start.8 = (f32[864,128]{1,0:T(8,128)S(1)}, f32[864,128]{1,0:T(8,128)S(1)}, u32[]{:S(2)}, u32[]{:S(2)}) collective-permute-start(f32[864,128]{1,0:T(8,128)S(1)} %collective-permute-done.7.refs_8_), channel_id=1, source_target_pairs={{0,1},{1,0},{2,3},{3,2},{4,5},{5,4},{6,7},{7,6},{8,9},{9,8},{10,11... | collective-permute-start | bytes 1327112 | tf_op jit(solution)/shard_map/cond/branch_0_fun/ppermute | solution.py:415
  92.1 33.2 %collective-permute-start.10 = (f32[864,128]{1,0:T(8,128)S(1)}, f32[864,128]{1,0:T(8,128)S(1)}, u32[]{:S(2)}, u32[]{:S(2)}) collective-permute-start(f32[864,128]{1,0:T(8,128)S(1)} %collective-permute-done.9.refs_10_), channel_id=1, source_target_pairs={{0,1},{1,0},{2,3},{3,2},{4,5},{5,4},{6,7},{7,6},{8,9},{9,8},{10,11... | collective-permute-start | bytes 1327112 | tf_op jit(solution)/shard_map/cond/branch_0_fun/ppermute | solution.py:415
  92.2 33.2 %collective-permute-start.14 = (f32[864,128]{1,0:T(8,128)S(1)}, f32[864,128]{1,0:T(8,128)S(1)}, u32[]{:S(2)}, u32[]{:S(2)}) collective-permute-start(f32[864,128]{1,0:T(8,128)S(1)} %collective-permute-done.13.refs_14_), channel_id=1, source_target_pairs={{0,1},{1,0},{2,3},{3,2},{4,5},{5,4},{6,7},{7,6},{8,9},{9,8},{10,11... | collective-permute-start | bytes 1327112 | tf_op jit(solution)/shard_map/cond/branch_0_fun/ppermute | solution.py:415
  92.7 32.7 %copy-start.2 = (f32[49,96,128]{2,1,0:T(8,128)S(1)}, f32[49,96,128]{2,1,0:T(8,128)}, u32[]{:S(2)}) copy-start(f32[49,96,128]{2,1,0:T(8,128)} %get-tuple-element.137.refs_20_) | copy-start | bytes 7225348 | tf_op jit(solution)/shard_map/cond
  92.7 32.7 %copy-start.5 = (bf16[256,256]{1,0:T(8,128)(2,1)S(1)}, bf16[256,256]{1,0:T(8,128)(2,1)}, u32[]{:S(2)}) copy-start(bf16[256,256]{1,0:T(8,128)(2,1)} %get-tuple-element.132.refs_16_) | copy-start | bytes 393220 | tf_op jit(solution)/shard_map/cond
  92.7 32.7 %copy-start.8 = (bf16[192,192]{1,0:T(8,128)(2,1)S(1)}, bf16[192,192]{1,0:T(8,128)(2,1)}, u32[]{:S(2)}) copy-start(bf16[192,192]{1,0:T(8,128)(2,1)} %get-tuple-element.133.refs_17_) | copy-start | bytes 221188 | tf_op jit(solution)/shard_map/cond
  162.9 3.6 %collective-permute-start.23 = (f32[864,128]{1,0:T(8,128)S(1)}, f32[864,128]{1,0:T(8,128)S(1)}, u32[]{:S(2)}, u32[]{:S(2)}) collective-permute-start(f32[864,128]{1,0:T(8,128)S(1)} %get-tuple-element.141), channel_id=1, source_target_pairs={{0,1},{1,0},{2,3},{3,2},{4,5},{5,4},{6,7},{7,6},{8,9},{9,8},{10,11... | collective-permute-start | bytes 1327112 | tf_op jit(solution)/shard_map/cond/branch_0_fun/ppermute | solution.py:415
  163.0 13.0 %collective-permute-start.24 = (f32[864,128]{1,0:T(8,128)S(1)}, f32[864,128]{1,0:T(8,128)S(1)}, u32[]{:S(2)}, u32[]{:S(2)}) collective-permute-start(f32[864,128]{1,0:T(8,128)S(1)} %get-tuple-element.142), channel_id=1, source_target_pairs={{0,2},{1,3},{2,0},{3,1},{4,6},{5,7},{6,4},{7,5},{8,10},{9,11},{10,... | collective-permute-start | bytes 1327112 | tf_op jit(solution)/shard_map/cond/branch_0_fun/ppermute | solution.py:415
  164.8 20.0 %collective-permute-start.25 = (f32[864,128]{1,0:T(8,128)S(1)}, f32[864,128]{1,0:T(8,128)S(1)}, u32[]{:S(2)}, u32[]{:S(2)}) collective-permute-start(f32[864,128]{1,0:T(8,128)S(1)} %get-tuple-element.143), channel_id=1, source_target_pairs={{0,3},{1,2},{2,1},{3,0},{4,7},{5,6},{6,5},{7,4},{8,11},{9,10},{10,... | collective-permute-start | bytes 1327112 | tf_op jit(solution)/shard_map/cond/branch_0_fun/ppermute | solution.py:415
  164.9 19.9 %collective-permute-start.26 = (f32[864,128]{1,0:T(8,128)S(1)}, f32[864,128]{1,0:T(8,128)S(1)}, u32[]{:S(2)}, u32[]{:S(2)}) collective-permute-start(f32[864,128]{1,0:T(8,128)S(1)} %get-tuple-element.144), channel_id=1, source_target_pairs={{0,4},{1,5},{2,6},{3,7},{4,0},{5,1},{6,2},{7,3},{8,12},{9,13},{10,... | collective-permute-start | bytes 1327112 | tf_op jit(solution)/shard_map/cond/branch_0_fun/ppermute | solution.py:415
  166.1 39.0 %collective-permute-start.27 = (f32[864,128]{1,0:T(8,128)S(1)}, f32[864,128]{1,0:T(8,128)S(1)}, u32[]{:S(2)}, u32[]{:S(2)}) collective-permute-start(f32[864,128]{1,0:T(8,128)S(1)} %get-tuple-element.145), channel_id=1, source_target_pairs={{0,5},{1,4},{2,7},{3,6},{4,1},{5,0},{6,3},{7,2},{8,13},{9,12},{10,... | collective-permute-start | bytes 1327112 | tf_op jit(solution)/shard_map/cond/branch_0_fun/ppermute | solution.py:415
  166.6 38.6 %collective-permute-start.28 = (f32[864,128]{1,0:T(8,128)S(1)}, f32[864,128]{1,0:T(8,128)S(1)}, u32[]{:S(2)}, u32[]{:S(2)}) collective-permute-start(f32[864,128]{1,0:T(8,128)S(1)} %get-tuple-element.146), channel_id=1, source_target_pairs={{0,6},{1,7},{2,4},{3,5},{4,2},{5,3},{6,0},{7,1},{8,14},{9,15},{10,... | collective-permute-start | bytes 1327112 | tf_op jit(solution)/shard_map/cond/branch_0_fun/ppermute | solution.py:415
  176.0 29.1 %collective-permute-start.29 = (f32[864,128]{1,0:T(8,128)S(1)}, f32[864,128]{1,0:T(8,128)S(1)}, u32[]{:S(2)}, u32[]{:S(2)}) collective-permute-start(f32[864,128]{1,0:T(8,128)S(1)} %get-tuple-element.147), channel_id=1, source_target_pairs={{0,7},{1,6},{2,5},{3,4},{4,3},{5,2},{6,1},{7,0},{8,15},{9,14},{10,... | collective-permute-start | bytes 1327112 | tf_op jit(solution)/shard_map/cond/branch_0_fun/ppermute | solution.py:415

commit v2 on v0

--- a/solution.py
+++ b/solution.py
@@ -1,13 +1,19 @@
+import functools
 import math
 
 import jax
 import jax.numpy as jnp
+import ml_dtypes
+import numpy as np
 from jax import lax
+from jax.experimental import pallas as pl
+from jax.experimental.pallas import tpu as pltpu
 from jax.sharding import PartitionSpec as P
 
 NX = 96
 NY = 96
 NZ = 96
+LANES = 128
 
 
 box_length = 16.0
@@ -41,7 +47,7 @@
     return shaped.reshape(count, planes, NY * NZ)
 
 
-def shards(orbitals, pair_mask, cycle_step):
+def slab_plan(orbitals, pair_mask, cycle_step):
     orbit_count = orbitals.shape[0]
     planes = orbitals.shape[1]
     grid_count = lax.axis_size("grid")
@@ -97,6 +103,395 @@
     return (exchange_field, projection)
 
 
+SLABS = 8
+GROUP = 4
+SLAB_PLANES = NX // SLABS
+COLS = NY * NZ // LANES
+SLAB_ROWS = SLAB_PLANES * COLS
+OCTETS = NY // 8
+UNROLL = (4, 4, 4)
+PAIR_VMEM = 36 << 20
+
+bf16 = jnp.bfloat16
+f32 = jnp.float32
+in_vmem = pl.BlockSpec(memory_space=pltpu.VMEM)
+in_smem = pl.BlockSpec(memory_space=pltpu.SMEM)
+
+
+def high_low(table):
+    high = table.astype(ml_dtypes.bfloat16)
+    return high, (table - high.astype(np.float64)).astype(ml_dtypes.bfloat16)
+
+
+def cas_table(length):
+    index = np.arange(length)
+    angle = (index[:, None] * index[None, :] % length) * (2.0 * np.pi / length)
+    return np.cos(angle) + np.sin(angle)
+
+
+def lane_table(table):
+    high, low = high_low(table)
+    out = np.zeros((2 * LANES, 2 * LANES), high.dtype)
+    for row in (0, LANES):
+        out[row : row + NZ, :NZ] = high
+        out[row : row + NZ, LANES : LANES + NZ] = low
+    return out
+
+
+def row_table(table):
+    high, low = high_low(table)
+    return np.concatenate([np.concatenate([high, high], 1), np.concatenate([low, low], 1)], 0)
+
+
+def plane_order(device):
+    return np.concatenate([np.arange(SLAB_PLANES) + SLAB_PLANES * (device ^ k) for k in range(SLABS)])
+
+
+def split(value):
+    high = value.astype(bf16)
+    return high, (value - high.astype(f32)).astype(bf16)
+
+
+def product(left, right):
+    return lax.dot_general(left, right, (((1,), (0,)), ((), ())), preferred_element_type=f32)
+
+
+def along_lanes(value, table):
+    both = product(jnp.concatenate(split(value), axis=1), table)
+    return both[:, :LANES] + both[:, LANES:]
+
+
+def along_rows(table, value):
+    both = product(table, jnp.concatenate(split(value), axis=0))
+    half = both.shape[0] // 2
+    return both[:half] + both[half:]
+
+
+def prepare_kernel(place, block, *refs):
+    outs, natural = refs[:-1], refs[-1]
+    me = place[0]
+
+    def two_columns(step, carry):
+        for a in range(GROUP):
+            pair = [block[:, a, pl.ds(pl.multiple_of((2 * step + i) * LANES, LANES), LANES)] for i in range(2)]
+            natural[a, pl.ds(pl.multiple_of(2 * SLAB_PLANES * step, 8), 2 * SLAB_PLANES), :] = jnp.concatenate(pair, 0)
+        return carry
+
+    lax.fori_loop(0, COLS // 2, two_columns, 0, unroll=2)
+    for k in range(GROUP):
+        outs[min(k, 2)][k // 3] = natural[(me & 3) ^ k]
+        outs[3 + k][0] = natural[((me >> 2) * 2) ^ k]
+
+
+def prepare(place, block):
+    slabs = [jax.ShapeDtypeStruct((count, SLAB_ROWS, LANES), f32) for count in (1, 1, 2, 1, 1, 1, 1)]
+    return pl.pallas_call(
+        prepare_kernel,
+        out_shape=slabs,
+        in_specs=[in_smem, in_vmem],
+        out_specs=[in_vmem] * 7,
+        scratch_shapes=[pltpu.VMEM((GROUP, SLAB_ROWS, LANES), f32)],
+        compiler_params=pltpu.CompilerParams(vmem_limit_bytes=32 << 20),
+        cost_estimate=pl.CostEstimate(flops=0, bytes_accessed=6 << 20, transcendentals=0),
+    )(place, block)
+
+
+def tables_kernel(place, lanes_in, rows_in, forward_in, back_in, table_z, table_y, table_x, table_back, coulomb, sems):
+    me = place[0]
+    copies = [
+        pltpu.make_async_copy(source, target, sems.at[i])
+        for i, (source, target) in enumerate(
+            ((lanes_in, table_z), (rows_in, table_y), (forward_in.at[me], table_x), (back_in.at[me], table_back))
+        )
+    ]
+    for copy in copies:
+        copy.start()
+    scale = box_length * box_length / math.pi / (NX * NY * NZ)
+    row = lax.broadcasted_iota(jnp.int32, (NY, LANES), 0)
+    lane = lax.broadcasted_iota(jnp.int32, (NY, LANES), 1)
+    plane = jnp.minimum(row, NY - row) ** 2 + jnp.minimum(lane, NZ - lane) ** 2
+    plane = plane.astype(f32)
+
+    def one_plane(x, carry):
+        squares = plane + (x * x).astype(f32)
+        coulomb[x] = jnp.where((squares > 0.5) & (lane < NZ), scale / jnp.maximum(squares, 1.0), 0.0)
+        return carry
+
+    lax.fori_loop(0, NX // 2 + 1, one_plane, 0)
+    for copy in copies:
+        copy.wait()
+
+
+def make_tables(place, tables):
+    return pl.pallas_call(
+        tables_kernel,
+        out_shape=[
+            jax.ShapeDtypeStruct(tables[0].shape, bf16),
+            *[jax.ShapeDtypeStruct(tables[1].shape, bf16)] * 3,
+            jax.ShapeDtypeStruct((NX // 2 + 1, NY, LANES), f32),
+        ],
+        in_specs=[in_smem] + [pl.BlockSpec(memory_space=pl.ANY)] * 4,
+        out_specs=[in_vmem] * 5,
+        scratch_shapes=[pltpu.SemaphoreType.DMA((4,))],
+        compiler_params=pltpu.CompilerParams(vmem_limit_bytes=16 << 20),
+        cost_estimate=pl.CostEstimate(flops=0, bytes_accessed=1 << 20, transcendentals=0),
+    )(place, *tables)
+
+
+OWN_PLACES = ((0, 0), (1, 0), (2, 0), (3, 1), (4, 0), (5, 0), (6, 0), (7, 1))
+VISITING_PLACES = (
+    ((0, 0), (1, 0), (2, 0), (3, 0), (0, 1), (1, 1), (2, 1), (3, 1)),
+    tuple((k, 0) for k in range(SLABS)),
+)
+
+
+def pair_kernel(turn, place, mask, *refs):
+    places = VISITING_PLACES[turn]
+    count = 1 + max(i for i, _ in places)
+    own_refs, vis_refs, refs = refs[:SLABS], refs[SLABS : SLABS + count], refs[SLABS + count :]
+    own_slabs = [own_refs[i].at[j] for i, j in OWN_PLACES]
+    vis_slabs = [vis_refs[i].at[j] for i, j in places]
+    table_z, table_y, table_x, table_back, coulomb, *refs = refs
+    if turn:
+        before, *refs = refs
+        outs, refs = refs[:SLABS], refs[SLABS:]
+    else:
+        out, *refs = refs
+    vis, spectrum = refs
+    me = place[0]
+    weight = -mask[me & 3, (me >> 2) * 2 + turn].astype(f32)
+
+    def rows_of(step):
+        return pl.ds(pl.multiple_of(2 * SLAB_PLANES * step, 8), 2 * SLAB_PLANES)
+
+    def columns_of(slabs, step):
+        pieces = [slab[rows_of(step), :] for slab in slabs]
+        return [
+            jnp.concatenate([piece[:SLAB_PLANES] for piece in pieces], axis=0),
+            jnp.concatenate([piece[SLAB_PLANES:] for piece in pieces], axis=0),
+        ]
+
+    def lane_index():
+        return lax.broadcasted_iota(jnp.int32, (NX, LANES), 1)
+
+    def forward(octet, carry):
+        lane = lane_index()
+        densities = []
+        for i in range(3):
+            step = 3 * octet + i
+            pair = columns_of(vis_slabs, step)
+            for j in range(2):
+                vis[2 * step + j] = pair[j]
+            densities += [a * b for a, b in zip(columns_of(own_slabs, step), pair)]
+        for q in range(2):
+            first, second, third = densities[3 * q : 3 * q + 3]
+            rows = [
+                first,
+                pltpu.roll(jnp.where(lane >= 96, first, second), 32, 1),
+                pltpu.roll(jnp.where(lane >= 64, second, third), 64, 1),
+                pltpu.roll(third, 96, 1),
+            ]
+            done = along_lanes(jnp.concatenate(rows, axis=0), table_z[...])
+            for j in range(2):
+                both = [done[(2 * j + i) * NX : (2 * j + i + 1) * NX] for i in range(2)]
+                both = along_rows(table_x[...], jnp.concatenate(both, axis=1))
+                at = 8 * octet + 4 * q + 2 * j
+                spectrum[at] = both[:, :LANES]
+                spectrum[at + 1] = both[:, LANES:]
+        return carry
+
+    lax.fori_loop(0, OCTETS, forward, 0, unroll=UNROLL[0])
+
+    def middle(step, carry):
+        base = pl.multiple_of(8 * step, 8)
+        block = jnp.swapaxes(spectrum[:, pl.ds(base, 8), :], 0, 1)
+        rows = []
+        for j in range(4):
+            both = along_rows(table_y[...], jnp.concatenate([block[2 * j], block[2 * j + 1]], axis=1))
+            at = [base + 2 * j, base + 2 * j + 1]
+            both = both * jnp.concatenate([coulomb[jnp.minimum(i, NX - i)] for i in at], axis=1)
+            both = along_rows(table_y[...], both)
+            rows += [both[:, :LANES], both[:, LANES:]]
+        spectrum[:, pl.ds(base, 8), :] = jnp.swapaxes(jnp.stack(rows, axis=0), 0, 1)
+        return carry
+
+    lax.fori_loop(0, NX // 8, middle, 0, unroll=UNROLL[1])
+
+    def back(octet, carry):
+        lane = lane_index()
+        values = []
+        for q in range(2):
+            rows = []
+            for j in range(2):
+                at = 8 * octet + 4 * q + 2 * j
+                both = along_rows(table_back[...], jnp.concatenate([spectrum[at], spectrum[at + 1]], axis=1))
+                rows += [both[:, :LANES], both[:, LANES:]]
+            done = along_lanes(jnp.concatenate(rows, axis=0), table_z[...])
+            first, second, third, fourth = [done[NX * i : NX * (i + 1)] for i in range(4)]
+            second = pltpu.roll(second, 96, 1)
+            third = pltpu.roll(third, 64, 1)
+            fourth = pltpu.roll(fourth, 32, 1)
+            columns = (
+                jnp.where(lane < 96, first, second),
+                jnp.where(lane < 64, second, third),
+                jnp.where(lane < 32, third, fourth),
+            )
+            for i in range(3):
+                at = 6 * octet + 3 * q + i
+                value = weight * (columns[i] * vis[at])
+                if turn:
+                    values.append(before[at] + value)
+                else:
+                    out[at] = value
+        if turn:
+            for i in range(3):
+                even, odd = values[2 * i : 2 * i + 2]
+                for k in range(SLABS):
+                    cut = slice(SLAB_PLANES * k, SLAB_PLANES * (k + 1))
+                    outs[k][rows_of(3 * octet + i), :] = jnp.concatenate([even[cut], odd[cut]], axis=0)
+        return carry
+
+    lax.fori_loop(0, OCTETS, back, 0, unroll=UNROLL[2])
+
+
+def pair_step(turn, place, mask, own, visiting, tables, before=None):
+    extra = [] if before is None else [before]
+    whole = jax.ShapeDtypeStruct((COLS, NX, LANES), f32)
+    slab = jax.ShapeDtypeStruct((SLAB_ROWS, LANES), f32)
+    return pl.pallas_call(
+        functools.partial(pair_kernel, turn),
+        out_shape=[slab] * SLABS if turn else whole,
+        in_specs=[in_smem] * 2 + [in_vmem] * (len(own) + len(visiting) + 5 + len(extra)),
+        out_specs=[in_vmem] * SLABS if turn else in_vmem,
+        scratch_shapes=[
+            pltpu.VMEM((COLS, NX, LANES), f32),
+            pltpu.VMEM((NY, NX, LANES), f32),
+        ],
+        compiler_params=pltpu.CompilerParams(vmem_limit_bytes=PAIR_VMEM),
+        cost_estimate=pl.CostEstimate(flops=0, bytes_accessed=1 << 20, transcendentals=0),
+    )(place, mask, *own, *visiting, *tables, *extra)
+
+
+def gram_kernel(place, *refs):
+    parts, refs = refs[:SLABS], refs[SLABS:]
+    own, refs = refs[:3], refs[3:]
+    natural, gram = refs
+    me = place[0] & 3
+    for k in range(GROUP):
+        natural[me ^ k] = parts[k][...] + parts[k + GROUP][...]
+    for a in range(GROUP):
+        for c in range(GROUP):
+            terms = own[min(a, 2)][a // 3] * natural[me ^ c]
+            terms = jnp.sum(terms.reshape(SLAB_ROWS // 8, 8, LANES), axis=0)
+            gram[(me ^ a) * GROUP + (me ^ c)] = jnp.sum(terms, axis=0, keepdims=True)
+
+
+def layout_kernel(natural, out):
+    def two_columns(step, carry):
+        rows = pl.ds(pl.multiple_of(2 * SLAB_PLANES * step, 8), 2 * SLAB_PLANES)
+        for a in range(GROUP):
+            pair = natural[a, rows, :]
+            for i in range(2):
+                lanes = pl.ds(pl.multiple_of((2 * step + i) * LANES, LANES), LANES)
+                out[:, a, lanes] = pair[SLAB_PLANES * i : SLAB_PLANES * (i + 1)]
+        return carry
+
+    lax.fori_loop(0, COLS // 2, two_columns, 0, unroll=2)
+
+
+def finish(place, parts, own):
+    natural, gram = pl.pallas_call(
+        gram_kernel,
+        out_shape=[
+            jax.ShapeDtypeStruct((GROUP, SLAB_ROWS, LANES), f32),
+            jax.ShapeDtypeStruct((GROUP * GROUP, 1, LANES), f32),
+        ],
+        in_specs=[in_smem] + [in_vmem] * (SLABS + 3),
+        out_specs=[in_vmem] * 2,
+        compiler_params=pltpu.CompilerParams(vmem_limit_bytes=32 << 20),
+        cost_estimate=pl.CostEstimate(flops=0, bytes_accessed=8 << 20, transcendentals=0),
+    )(place, *parts, *own)
+    field = pl.pallas_call(
+        layout_kernel,
+        out_shape=jax.ShapeDtypeStruct((SLAB_PLANES, GROUP, NY * NZ), f32),
+        in_specs=[in_vmem],
+        out_specs=in_vmem,
+        compiler_params=pltpu.CompilerParams(vmem_limit_bytes=32 << 20),
+        cost_estimate=pl.CostEstimate(flops=0, bytes_accessed=8 << 20, transcendentals=0),
+    )(natural)
+    gram = jnp.sum(gram.reshape(GROUP, GROUP, LANES), axis=2) / (NX * NY * NZ)
+    for flip in (1, 2, 4):
+        gram = gram + to_partner(gram, flip)
+    return field, gram
+
+
+def to_partner(block, flip):
+    return lax.ppermute(block, "grid", [(i, i ^ flip) for i in range(SLABS)])
+
+
+def to_group(block, distance, flip):
+    bands = lax.axis_size("band")
+    route = [(b * SLABS + i, (b + distance) % bands * SLABS + (i ^ flip)) for b in range(bands) for i in range(SLABS)]
+    return lax.ppermute(block, ("band", "grid"), route)
+
+
+def after(value, *others):
+    return lax.optimization_barrier((value, *others))[0]
+
+
+def pair_plan(orbitals, pair_mask, cycle_step):
+    me = lax.axis_index("grid")
+    place = me.astype(jnp.int32).reshape(1)
+    cas = cas_table(NX)
+    forward_x = jnp.asarray(np.stack([row_table(cas[:, plane_order(d)]) for d in range(SLABS)]))
+    back_x = jnp.asarray(np.stack([row_table(cas[plane_order(d), :]) for d in range(SLABS)]))
+    fixed = jnp.asarray(lane_table(cas)), jnp.asarray(row_table(cas)), forward_x, back_x
+    slabs = prepare(place, jnp.transpose(orbitals, (1, 0, 2)))
+
+    def with_distance(distance, slabs, pair_mask, place, fixed):
+        own_out, vis_out = slabs[:3], slabs[3:]
+        home = to_group(vis_out[0], distance, 0)
+        across = to_group(vis_out[2], distance, 4)
+        own_y = to_partner(own_out[0], 4)
+        own_x = to_partner(own_out[2], 2)
+        own_next = to_partner(own_out[1], 4)
+        first = jnp.concatenate([after(home, own_x, own_y), across])
+        first_x = to_partner(first, 2)
+        home = to_group(after(vis_out[1], first), distance, 0)
+        across = to_group(after(vis_out[3], first), distance, 4)
+        tables = make_tables(after(place, first), fixed)
+        own_far = to_partner(after(own_x, across, own_next, *tables), 4)
+        home_x, across_x = to_partner(home, 2), to_partner(across, 2)
+        cores = [to_partner(after(array, home), 1) for array in (own_out[1], own_x, own_next)]
+        cores.append(to_partner(after(own_far, home_x), 1))
+        own = [own_out[0], cores[0], own_x, cores[1], own_y, cores[2], own_far, cores[3]]
+        visiting = [first, to_partner(after(first, home), 1), first_x, to_partner(after(first_x, home), 1)]
+        total = pair_step(0, place, pair_mask, own, visiting, tables)
+        cores = [to_partner(slab, 1) for slab in (home, home_x, across)]
+        cores.append(to_partner(after(across_x, total), 1))
+        visiting = [home, cores[0], home_x, cores[1], across, cores[2], across_x, cores[3]]
+        parts = pair_step(1, place, pair_mask, own, visiting, tables, total)
+        parts = [parts[0]] + [to_partner(parts[k], k) for k in range(1, SLABS)]
+        return finish(place, parts, own_out)
+
+    bands = lax.axis_size("band")
+    field, gram = lax.switch(
+        cycle_step - 1,
+        [functools.partial(with_distance, distance) for distance in range(1, bands)],
+        slabs,
+        pair_mask,
+        place,
+        fixed,
+    )
+    return jnp.transpose(field, (1, 0, 2)), gram
+
+
+def shards(orbitals, pair_mask, cycle_step):
+    if lax.axis_size("grid") == SLABS and orbitals.shape[0] == GROUP:
+        return pair_plan(orbitals, pair_mask, cycle_step)
+    return slab_plan(orbitals, pair_mask, cycle_step)
+
+
 def solution(mesh):
     return jax.shard_map(
         shards,

time: 902 us -> 156 us (0.17); the launches traced: 916 us -> 157 us
  local copies, waits for them, and re-layouts: 407 us -> 2.83 us
  waiting for transfers between devices: 282 us -> 92.8 us
  matrix products: 109 us -> 0 us
  other arithmetic: 89.3 us -> 0.22 us
  Pallas kernels: 0 us -> 32 us
  starting transfers between devices: 13.3 us -> 27.3 us
  blocking collectives: 11.8 us -> 0 us
    unnamed x14, local copies, waits for them, and re-layouts: 238 us -> 2.68 us
    all_to_all x2 -> x0, waiting for transfers between devices: 159 us -> none  [the longest x1 80 us: solve_items(): lax.all_to_all(along, 'grid', split_axis=1, concat_axis=2, tiled=True)]
    dot_general x8 -> x0, matrix products: 109 us -> none  [the longest x2 47.3 us: across_planes(): shaped = jnp.matmul(shaped, table_z, precision=highest)]
    all_to_all x1 -> x0, other arithmetic: 76.3 us -> none  [one_group(): lax.all_to_all(spectra, 'grid', split_axis=2, concat_axis=1, tiled=True)]
    reshape x3 -> x0, local copies, waits for them, and re-layouts: 73.6 us -> none  [the longest x2 62.2 us: across_planes(): return shaped.reshape(count, planes, NY * NZ)]
    all_to_all x3 -> x0, local copies, waits for them, and re-layouts: 54.8 us -> none  [the longest x2 44.8 us: one_group(): lax.all_to_all(spectra, 'grid', split_axis=2, concat_axis=1, tiled=True)]
    pallas_call x0 -> x6, Pallas kernels: none -> 32 us  [the longest x2 26.1 us: pair_step(): pl.pallas_call(functools.partial(pair_kernel, turn), out_shape=[slab] * S...]
    ppermute x3 -> x31, waiting for transfers between devices: 123 us -> 92.8 us  [the longest x27 85 us: to_partner(): return lax.ppermute(block, 'grid', [(i, i ^ flip) for i in range(SLABS)])]
  transfers between devices with their start and end apart: 5 -> 31, of which waited for: 5 -> 15; matrix products, arithmetic and copies ran while one was open for 0% -> 0% of each run, Pallas kernels for 0% -> 10%
where the time goes in v2:
time: 156 us; the launch traced here: 157 us
  waiting for transfers between devices  92.8 us (59%)
  Pallas kernels  32 us (21%)
  starting transfers between devices  27.3 us (18%)
  local copies, waits for them, and re-layouts  2.83 us (2%)
    ppermute x27, waiting for transfers between devices, to_partner(): return lax.ppermute(block, 'grid', [(i, i ^ flip) for i in range(SLABS)])  85 us
    pallas_call x2, Pallas kernels, pair_step(): pl.pallas_call(functools.partial(pair_kernel, turn), out_shape=[slab] * S...  26.1 us
    ppermute x27, starting transfers between devices, to_partner(): return lax.ppermute(block, 'grid', [(i, i ^ flip) for i in range(SLABS)])  21.4 us
    ppermute x4, waiting for transfers between devices, to_group(): return lax.ppermute(block, ('band', 'grid'), route)  7.75 us
    ppermute x4, starting transfers between devices, to_group(): return lax.ppermute(block, ('band', 'grid'), route)  5.9 us
  transfers between devices with their start and end apart: 31, of which 15 were waited for; matrix products, arithmetic and copies ran while one was open for 0% of the time, Pallas kernels for 10%

profile of v2, /device:TPU:0, one launch (start us, length us, event | category | flops | bytes accessed | tf_op | source)
XLA Modules:
  0.0 156.9 jit_solution(11283842013573281559)
XLA Ops:
  1.3 1.5 copy-done
  2.8 1.5 shard_map.86
  4.3 151.3 %conditional.1 = (f32[12,4,9216]{2,1,0:T(4,128)S(1)}, f32[4,4]{1,0:T(4,128)S(1)}) conditional(s32[]{:T(128)} %clamp.3, (f32[1,864,128]{2,1,0:T(8,128)S(1)}, f32[2,864,128]{2,1,0:T(8,128)S(1)}, f32[1,864,128]{2,1,0:T(8,128)S(1)}, f32[1,864,128]{2,1,0:T(8,128)S(1)}, f32[1,864,128]{2,1,0:T(8,128)S(1)}, ...), branch_computations={%region_0.0_spmd, %region_2.0_spmd, %region_4.0_spmd} | conditional | flops 2096 | bytes 83929992 | solution.py:478
  4.6 3.0 %collective-permute-start.63 = (f32[2,864,128]{2,1,0:T(8,128)S(1)}, f32[2,864,128]{2,1,0:T(8,128)S(1)}, u32[]{:S(2)}, u32[]{:S(2)}) collective-permute-start(f32[2,864,128]{2,1,0:T(8,128)S(1)} %get-tuple-element.164.refs_10_), channel_id=1, source_target_pairs={{0,2},{1,3},{2,0},{3,1},{4,6},{5,7},{6,4},{7,5},{8,10},{9,11},{10,... | collective-permute-start | bytes 2654216 | tf_op jit(solution)/shard_map/cond/branch_2_fun/ppermute | solution.py:429
  7.6 3.6 %collective-permute-start.62 = (f32[1,864,128]{2,1,0:T(8,128)S(1)}, f32[1,864,128]{2,1,0:T(8,128)S(1)}, u32[]{:S(2)}, u32[]{:S(2)}) collective-permute-start(f32[1,864,128]{2,1,0:T(8,128)S(1)} %get-tuple-element.163), channel_id=1, source_target_pairs={{0,24},{1,25},{2,26},{3,27},{4,28},{5,29},{6,30},{7,31},{8,0},{9,1... | collective-permute-start | bytes 1327112 | tf_op jit(solution)/shard_map/cond/branch_2_fun/ppermute | solution.py:435
  11.2 1.5 collective-permute-start.64
  12.7 0.4 collective-permute-start.65
  13.1 1.5 collective-permute-start.69
  14.6 7.2 %collective-permute-done.62 = f32[1,864,128]{2,1,0:T(8,128)S(1)} collective-permute-done((f32[1,864,128]{2,1,0:T(8,128)S(1)}, f32[1,864,128]{2,1,0:T(8,128)S(1)}, u32[]{:S(2)}, u32[]{:S(2)}) %collective-permute-start.62) | collective-permute-done | bytes 442400 | tf_op jit(solution)/shard_map/cond/branch_2_fun/ppermute | solution.py:435
  21.8 12.0 %collective-permute-done.64.refs_4_ = f32[1,864,128]{2,1,0:T(8,128)S(1)} collective-permute-done((f32[1,864,128]{2,1,0:T(8,128)S(1)}, f32[1,864,128]{2,1,0:T(8,128)S(1)}, u32[]{:S(2)}, u32[]{:S(2)}) %collective-permute-start.64) | collective-permute-done | bytes 442400 | tf_op jit(solution)/shard_map/cond/branch_2_fun/ppermute | solution.py:429
  33.8 1.5 collective-permute-start.71
  35.3 0.5 collective-permute-start.80
  35.8 0.4 collective-permute-start.66
  36.3 1.5 branch_2_fun.5
  37.8 13.2 %collective-permute-done.69 = f32[1,864,128]{2,1,0:T(8,128)S(1)} collective-permute-done((f32[1,864,128]{2,1,0:T(8,128)S(1)}, f32[1,864,128]{2,1,0:T(8,128)S(1)}, u32[]{:S(2)}, u32[]{:S(2)}) %collective-permute-start.69) | collective-permute-done | bytes 442400 | tf_op jit(solution)/shard_map/cond/branch_2_fun/ppermute | solution.py:429
  51.0 1.5 collective-permute-start.72
  52.5 0.6 collective-permute-done.66.refs_8_
  53.0 0.5 collective-permute-start.73
  53.6 0.5 collective-permute-start.68
  54.1 2.6 %collective-permute-done.80.refs_10_ = f32[2,864,128]{2,1,0:T(8,128)S(1)} collective-permute-done((f32[2,864,128]{2,1,0:T(8,128)S(1)}, f32[2,864,128]{2,1,0:T(8,128)S(1)}, u32[]{:S(2)}, u32[]{:S(2)}) %collective-permute-start.80) | collective-permute-done | bytes 884768 | tf_op jit(solution)/shard_map/cond/branch_2_fun/ppermute | solution.py:429
  56.7 7.7 %collective-permute-done.73.refs_10_ = f32[1,864,128]{2,1,0:T(8,128)S(1)} collective-permute-done((f32[1,864,128]{2,1,0:T(8,128)S(1)}, f32[1,864,128]{2,1,0:T(8,128)S(1)}, u32[]{:S(2)}, u32[]{:S(2)}) %collective-permute-start.73) | collective-permute-done | bytes 442400 | tf_op jit(solution)/shard_map/cond/branch_2_fun/ppermute | solution.py:429
  64.5 6.4 %collective-permute-done.72.refs_6_ = f32[2,864,128]{2,1,0:T(8,128)S(1)} collective-permute-done((f32[2,864,128]{2,1,0:T(8,128)S(1)}, f32[2,864,128]{2,1,0:T(8,128)S(1)}, u32[]{:S(2)}, u32[]{:S(2)}) %collective-permute-start.72) | collective-permute-done | bytes 884768 | tf_op jit(solution)/shard_map/cond/branch_2_fun/ppermute | solution.py:429
  70.9 0.5 collective-permute-start.70
  71.4 2.5 %collective-permute-done.70.refs_5_ = f32[1,864,128]{2,1,0:T(8,128)S(1)} collective-permute-done((f32[1,864,128]{2,1,0:T(8,128)S(1)}, f32[1,864,128]{2,1,0:T(8,128)S(1)}, u32[]{:S(2)}, u32[]{:S(2)}) %collective-permute-start.70) | collective-permute-done | bytes 442400 | tf_op jit(solution)/shard_map/cond/branch_2_fun/ppermute | solution.py:429
  73.9 0.5 collective-permute-start.78
  74.5 0.5 collective-permute-start.77
  75.0 13.0 %branch_2_fun.6.refs_21_ = f32[72,96,128]{2,1,0:T(8,128)S(1)} custom-call(s32[1]{0:T(128)} %get-tuple-element.173.place, s32[4,4]{1,0:T(4,128)S(1)} %get-tuple-element.159.mask, f32[1,864,128]{2,1,0:T(8,128)S(1)} %get-tuple-element.160.refs_0_.refs_8_, f32[1,864,128]{2,1,0:T(8,128)S(1)} %collective-permute-done.67.refs_1_, ...), custom_call_target="tpu_custom_call" | custom-call | bytes 1048576 | tf_op jit(solution)/shard_map/cond/branch_2_fun/pallas_call | solution.py:361
  88.1 0.5 collective-permute-start.82
  88.6 1.4 collective-permute-done.82.refs_15_
  90.0 13.1 %branch_2_fun.7 = (f32[864,128]{1,0:T(8,128)S(1)}, f32[864,128]{1,0:T(8,128)S(1)}, f32[864,128]{1,0:T(8,128)S(1)}, f32[864,128]{1,0:T(8,128)S(1)}, f32[864,128]{...) custom-call(s32[1]{0:T(128)} %get-tuple-element.173.place, ...), custom_call_target="tpu_custom_call" | custom-call | bytes 1048576 | tf_op jit(solution)/shard_map/cond/branch_2_fun/pallas_call | solution.py:361
  103.1 0.4 collective-permute-start.83
  103.5 1.5 collective-permute-start.84
  105.0 1.5 collective-permute-start.86
  106.6 0.5 collective-permute-start.87
  107.0 2.5 %collective-permute-start.88 = (f32[864,128]{1,0:T(8,128)S(1)}, f32[864,128]{1,0:T(8,128)S(1)}, u32[]{:S(2)}, u32[]{:S(2)}) collective-permute-start(f32[864,128]{1,0:T(8,128)S(1)} %get-tuple-element.194), channel_id=1, source_target_pairs={{0,6},{1,7},{2,4},{3,5},{4,2},{5,3},{6,0},{7,1},{8,14},{9,15},{10,... | collective-permute-start | bytes 1327112 | tf_op jit(solution)/shard_map/cond/branch_2_fun/ppermute | solution.py:429
  109.5 7.0 %collective-permute-done.84.refs_2_ = f32[864,128]{1,0:T(8,128)S(1)} collective-permute-done((f32[864,128]{1,0:T(8,128)S(1)}, f32[864,128]{1,0:T(8,128)S(1)}, u32[]{:S(2)}, u32[]{:S(2)}) %collective-permute-start.84) | collective-permute-done | bytes 442400 | tf_op jit(solution)/shard_map/cond/branch_2_fun/ppermute | solution.py:429
  116.5 0.5 collective-permute-start.89
  117.0 8.0 %collective-permute-done.85.refs_3_ = f32[864,128]{1,0:T(8,128)S(1)} collective-permute-done((f32[864,128]{1,0:T(8,128)S(1)}, f32[864,128]{1,0:T(8,128)S(1)}, u32[]{:S(2)}, u32[]{:S(2)}) %collective-permute-start.85) | collective-permute-done | bytes 442400 | tf_op jit(solution)/shard_map/cond/branch_2_fun/ppermute | solution.py:429
  125.1 20.9 %collective-permute-done.87.refs_5_ = f32[864,128]{1,0:T(8,128)S(1)} collective-permute-done((f32[864,128]{1,0:T(8,128)S(1)}, f32[864,128]{1,0:T(8,128)S(1)}, u32[]{:S(2)}, u32[]{:S(2)}) %collective-permute-start.87) | collective-permute-done | bytes 442400 | tf_op jit(solution)/shard_map/cond/branch_2_fun/ppermute | solution.py:429
  145.9 1.0 branch_2_fun.8
  146.9 0.2 reduce_sum.26
  147.3 1.0 collective-permute-done.90
  148.4 1.5 collective-permute-start.91
  149.9 2.1 %collective-permute-done.91 = f32[4,4]{1,0:T(4,128)S(1)} collective-permute-done((f32[4,4]{1,0:T(4,128)S(1)}, f32[4,4]{1,0:T(4,128)S(1)}, u32[]{:S(2)}, u32[]{:S(2)}) %collective-permute-start.91) | collective-permute-done | bytes 96 | tf_op jit(solution)/shard_map/cond/branch_2_fun/ppermute | solution.py:429
  152.0 1.5 collective-permute-start.92
  153.5 1.9 %branch_2_fun.9 = f32[12,4,9216]{2,1,0:T(4,128)S(1)} custom-call(f32[4,864,128]{2,1,0:T(8,128)S(1)} %get-tuple-element.196.natural), custom_call_target="tpu_custom_call" | custom-call | bytes 8388608 | tf_op jit(solution)/shard_map/cond/branch_2_fun/pallas_call | solution.py:414
  155.4 0.1 collective-permute-done.92
  155.7 1.2 copy-done.3
  (45 shorter events, 0.4 us)
Async XLA Ops:
  0.6 3.7 %copy-start.8 = (s32[4,4]{1,0:T(4,128)S(1)}, s32[4,4]{1,0:T(4,128)}, u32[]{:S(2)}) copy-start(s32[4,4]{1,0:T(4,128)} %param.11) | copy-start | bytes 196
  1.3 1.5 copy-start
  2.8 1.5 copy-start.1
  2.8 1.5 copy-start.2
  2.8 1.5 copy-start.4
  4.5 31.7 %copy-start.7 = (bf16[192,192]{1,0:T(8,128)(2,1)S(1)}, bf16[192,192]{1,0:T(8,128)(2,1)}, u32[]{:S(2)}) copy-start(bf16[192,192]{1,0:T(8,128)(2,1)} %get-tuple-element.175.rows_in) | copy-start | bytes 221188 | tf_op jit(solution)/shard_map/cond
  4.6 29.2 %collective-permute-start.63 = (f32[2,864,128]{2,1,0:T(8,128)S(1)}, f32[2,864,128]{2,1,0:T(8,128)S(1)}, u32[]{:S(2)}, u32[]{:S(2)}) collective-permute-start(f32[2,864,128]{2,1,0:T(8,128)S(1)} %get-tuple-element.164.refs_10_), channel_id=1, source_target_pairs={{0,2},{1,3},{2,0},{3,1},{4,6},{5,7},{6,4},{7,5},{8,10},{9,11},{10,... | collective-permute-start | bytes 2654216 | tf_op jit(solution)/shard_map/cond/branch_2_fun/ppermute | solution.py:429
  7.6 14.2 %collective-permute-start.62 = (f32[1,864,128]{2,1,0:T(8,128)S(1)}, f32[1,864,128]{2,1,0:T(8,128)S(1)}, u32[]{:S(2)}, u32[]{:S(2)}) collective-permute-start(f32[1,864,128]{2,1,0:T(8,128)S(1)} %get-tuple-element.163), channel_id=1, source_target_pairs={{0,24},{1,25},{2,26},{3,27},{4,28},{5,29},{6,30},{7,31},{8,0},{9,1... | collective-permute-start | bytes 1327112 | tf_op jit(solution)/shard_map/cond/branch_2_fun/ppermute | solution.py:435
  11.2 22.6 %collective-permute-start.64 = (f32[1,864,128]{2,1,0:T(8,128)S(1)}, f32[1,864,128]{2,1,0:T(8,128)S(1)}, u32[]{:S(2)}, u32[]{:S(2)}) collective-permute-start(f32[1,864,128]{2,1,0:T(8,128)S(1)} %get-tuple-element.160.refs_0_.refs_8_), channel_id=1, source_target_pairs={{0,4},{1,5},{2,6},{3,7},{4,0},{5,1},{6,2},{7,3},{8,12},{9,13},{10,... | collective-permute-start | bytes 1327112 | tf_op jit(solution)/shard_map/cond/branch_2_fun/ppermute | solution.py:429
  12.7 21.1 %collective-permute-start.65 = (f32[1,864,128]{2,1,0:T(8,128)S(1)}, f32[1,864,128]{2,1,0:T(8,128)S(1)}, u32[]{:S(2)}, u32[]{:S(2)}) collective-permute-start(f32[1,864,128]{2,1,0:T(8,128)S(1)} %get-tuple-element.166), channel_id=1, source_target_pairs={{0,28},{1,29},{2,30},{3,31},{4,24},{5,25},{6,26},{7,27},{8,4},{9,5... | collective-permute-start | bytes 1327112 | tf_op jit(solution)/shard_map/cond/branch_2_fun/ppermute | solution.py:435
  13.1 37.9 %collective-permute-start.69 = (f32[1,864,128]{2,1,0:T(8,128)S(1)}, f32[1,864,128]{2,1,0:T(8,128)S(1)}, u32[]{:S(2)}, u32[]{:S(2)}) collective-permute-start(f32[1,864,128]{2,1,0:T(8,128)S(1)} %get-tuple-element.168.refs_9_), channel_id=1, source_target_pairs={{0,4},{1,5},{2,6},{3,7},{4,0},{5,1},{6,2},{7,3},{8,12},{9,13},{10,... | collective-permute-start | bytes 1327112 | tf_op jit(solution)/shard_map/cond/branch_2_fun/ppermute | solution.py:429
  33.8 17.1 %collective-permute-start.71 = (f32[1,864,128]{2,1,0:T(8,128)S(1)}, f32[1,864,128]{2,1,0:T(8,128)S(1)}, u32[]{:S(2)}, u32[]{:S(2)}) collective-permute-start(f32[1,864,128]{2,1,0:T(8,128)S(1)} %get-tuple-element.172), channel_id=1, source_target_pairs={{0,28},{1,29},{2,30},{3,31},{4,24},{5,25},{6,26},{7,27},{8,4},{9,5... | collective-permute-start | bytes 1327112 | tf_op jit(solution)/shard_map/cond/branch_2_fun/ppermute | solution.py:435
  35.3 21.4 %collective-permute-start.80 = (f32[2,864,128]{2,1,0:T(8,128)S(1)}, f32[2,864,128]{2,1,0:T(8,128)S(1)}, u32[]{:S(2)}, u32[]{:S(2)}) collective-permute-start(f32[2,864,128]{2,1,0:T(8,128)S(1)} %constant_dynamic-update-slice_fusion.4.refs_8_), channel_id=1, source_target_pairs={{0,2},{1,3},{2,0},{3,1},{4,6},{5,7},{6,4},{7,5},{8,10},{9,11},{10,... | collective-permute-start | bytes 2654216 | tf_op jit(solution)/shard_map/cond/branch_2_fun/ppermute | solution.py:429
  35.8 17.2 %collective-permute-start.66 = (f32[1,864,128]{2,1,0:T(8,128)S(1)}, f32[1,864,128]{2,1,0:T(8,128)S(1)}, u32[]{:S(2)}, u32[]{:S(2)}) collective-permute-start(f32[1,864,128]{2,1,0:T(8,128)S(1)} %get-tuple-element.167), channel_id=1, source_target_pairs={{0,24},{1,25},{2,26},{3,27},{4,28},{5,29},{6,30},{7,31},{8,0},{9,1... | collective-permute-start | bytes 1327112 | tf_op jit(solution)/shard_map/cond/branch_2_fun/ppermute | solution.py:435
  51.0 19.9 %collective-permute-start.72 = (f32[2,864,128]{2,1,0:T(8,128)S(1)}, f32[2,864,128]{2,1,0:T(8,128)S(1)}, u32[]{:S(2)}, u32[]{:S(2)}) collective-permute-start(f32[2,864,128]{2,1,0:T(8,128)S(1)} %collective-permute-done.63.refs_2_), channel_id=1, source_target_pairs={{0,4},{1,5},{2,6},{3,7},{4,0},{5,1},{6,2},{7,3},{8,12},{9,13},{10,... | collective-permute-start | bytes 2654216 | tf_op jit(solution)/shard_map/cond/branch_2_fun/ppermute | solution.py:429
  53.0 11.4 %collective-permute-start.73 = (f32[1,864,128]{2,1,0:T(8,128)S(1)}, f32[1,864,128]{2,1,0:T(8,128)S(1)}, u32[]{:S(2)}, u32[]{:S(2)}) collective-permute-start(f32[1,864,128]{2,1,0:T(8,128)S(1)} %collective-permute-done.66.refs_8_), channel_id=1, source_target_pairs={{0,2},{1,3},{2,0},{3,1},{4,6},{5,7},{6,4},{7,5},{8,10},{9,11},{10,... | collective-permute-start | bytes 1327112 | tf_op jit(solution)/shard_map/cond/branch_2_fun/ppermute | solution.py:429
  53.6 17.3 %collective-permute-start.67 = (f32[1,864,128]{2,1,0:T(8,128)S(1)}, f32[1,864,128]{2,1,0:T(8,128)S(1)}, u32[]{:S(2)}, u32[]{:S(2)}) collective-permute-start(f32[1,864,128]{2,1,0:T(8,128)S(1)} %get-tuple-element.168.refs_9_), channel_id=1, source_target_pairs={{0,1},{1,0},{2,3},{3,2},{4,5},{5,4},{6,7},{7,6},{8,9},{9,8},{10,11... | collective-permute-start | bytes 1327112 | tf_op jit(solution)/shard_map/cond/branch_2_fun/ppermute | solution.py:429
  53.6 20.9 %collective-permute-start.68 = (f32[2,864,128]{2,1,0:T(8,128)S(1)}, f32[2,864,128]{2,1,0:T(8,128)S(1)}, u32[]{:S(2)}, u32[]{:S(2)}) collective-permute-start(f32[2,864,128]{2,1,0:T(8,128)S(1)} %collective-permute-done.63.refs_2_), channel_id=1, source_target_pairs={{0,1},{1,0},{2,3},{3,2},{4,5},{5,4},{6,7},{7,6},{8,9},{9,8},{10,11... | collective-permute-start | bytes 2654216 | tf_op jit(solution)/shard_map/cond/branch_2_fun/ppermute | solution.py:429
  56.7 17.7 %collective-permute-start.79 = (f32[2,864,128]{2,1,0:T(8,128)S(1)}, f32[2,864,128]{2,1,0:T(8,128)S(1)}, u32[]{:S(2)}, u32[]{:S(2)}) collective-permute-start(f32[2,864,128]{2,1,0:T(8,128)S(1)} %constant_dynamic-update-slice_fusion.4.refs_8_), channel_id=1, source_target_pairs={{0,1},{1,0},{2,3},{3,2},{4,5},{5,4},{6,7},{7,6},{8,9},{9,8},{10,11... | collective-permute-start | bytes 2654216 | tf_op jit(solution)/shard_map/cond/branch_2_fun/ppermute | solution.py:429
  64.5 10.5 %collective-permute-start.81 = (f32[2,864,128]{2,1,0:T(8,128)S(1)}, f32[2,864,128]{2,1,0:T(8,128)S(1)}, u32[]{:S(2)}, u32[]{:S(2)}) collective-permute-start(f32[2,864,128]{2,1,0:T(8,128)S(1)} %collective-permute-done.80.refs_10_), channel_id=1, source_target_pairs={{0,1},{1,0},{2,3},{3,2},{4,5},{5,4},{6,7},{7,6},{8,9},{9,8},{10,11... | collective-permute-start | bytes 2654216 | tf_op jit(solution)/shard_map/cond/branch_2_fun/ppermute | solution.py:429
  70.9 4.2 %collective-permute-start.74 = (f32[2,864,128]{2,1,0:T(8,128)S(1)}, f32[2,864,128]{2,1,0:T(8,128)S(1)}, u32[]{:S(2)}, u32[]{:S(2)}) collective-permute-start(f32[2,864,128]{2,1,0:T(8,128)S(1)} %collective-permute-done.72.refs_6_), channel_id=1, source_target_pairs={{0,1},{1,0},{2,3},{3,2},{4,5},{5,4},{6,7},{7,6},{8,9},{9,8},{10,11... | collective-permute-start | bytes 2654216 | tf_op jit(solution)/shard_map/cond/branch_2_fun/ppermute | solution.py:429
  70.9 3.1 %collective-permute-start.70 = (f32[1,864,128]{2,1,0:T(8,128)S(1)}, f32[1,864,128]{2,1,0:T(8,128)S(1)}, u32[]{:S(2)}, u32[]{:S(2)}) collective-permute-start(f32[1,864,128]{2,1,0:T(8,128)S(1)} %collective-permute-done.69), channel_id=1, source_target_pairs={{0,1},{1,0},{2,3},{3,2},{4,5},{5,4},{6,7},{7,6},{8,9},{9,8},{10,11... | collective-permute-start | bytes 1327112 | tf_op jit(solution)/shard_map/cond/branch_2_fun/ppermute | solution.py:429
  73.9 14.2 %collective-permute-start.78 = (f32[1,864,128]{2,1,0:T(8,128)S(1)}, f32[1,864,128]{2,1,0:T(8,128)S(1)}, u32[]{:S(2)}, u32[]{:S(2)}) collective-permute-start(f32[1,864,128]{2,1,0:T(8,128)S(1)} %collective-permute-done.71.refs_12_), channel_id=1, source_target_pairs={{0,2},{1,3},{2,0},{3,1},{4,6},{5,7},{6,4},{7,5},{8,10},{9,11},{10,... | collective-permute-start | bytes 1327112 | tf_op jit(solution)/shard_map/cond/branch_2_fun/ppermute | solution.py:429
  74.5 14.1 %collective-permute-start.75 = (f32[1,864,128]{2,1,0:T(8,128)S(1)}, f32[1,864,128]{2,1,0:T(8,128)S(1)}, u32[]{:S(2)}, u32[]{:S(2)}) collective-permute-start(f32[1,864,128]{2,1,0:T(8,128)S(1)} %collective-permute-done.66.refs_8_), channel_id=1, source_target_pairs={{0,1},{1,0},{2,3},{3,2},{4,5},{5,4},{6,7},{7,6},{8,9},{9,8},{10,11... | collective-permute-start | bytes 1327112 | tf_op jit(solution)/shard_map/cond/branch_2_fun/ppermute | solution.py:429
  74.5 14.1 %collective-permute-start.77 = (f32[1,864,128]{2,1,0:T(8,128)S(1)}, f32[1,864,128]{2,1,0:T(8,128)S(1)}, u32[]{:S(2)}, u32[]{:S(2)}) collective-permute-start(f32[1,864,128]{2,1,0:T(8,128)S(1)} %collective-permute-done.71.refs_12_), channel_id=1, source_target_pairs={{0,1},{1,0},{2,3},{3,2},{4,5},{5,4},{6,7},{7,6},{8,9},{9,8},{10,11... | collective-permute-start | bytes 1327112 | tf_op jit(solution)/shard_map/cond/branch_2_fun/ppermute | solution.py:429
  75.0 13.6 %collective-permute-start.76 = (f32[1,864,128]{2,1,0:T(8,128)S(1)}, f32[1,864,128]{2,1,0:T(8,128)S(1)}, u32[]{:S(2)}, u32[]{:S(2)}) collective-permute-start(f32[1,864,128]{2,1,0:T(8,128)S(1)} %collective-permute-done.73.refs_10_), channel_id=1, source_target_pairs={{0,1},{1,0},{2,3},{3,2},{4,5},{5,4},{6,7},{7,6},{8,9},{9,8},{10,11... | collective-permute-start | bytes 1327112 | tf_op jit(solution)/shard_map/cond/branch_2_fun/ppermute | solution.py:429
  88.1 1.9 %collective-permute-start.82 = (f32[1,864,128]{2,1,0:T(8,128)S(1)}, f32[1,864,128]{2,1,0:T(8,128)S(1)}, u32[]{:S(2)}, u32[]{:S(2)}) collective-permute-start(f32[1,864,128]{2,1,0:T(8,128)S(1)} %collective-permute-done.78.refs_14_), channel_id=1, source_target_pairs={{0,1},{1,0},{2,3},{3,2},{4,5},{5,4},{6,7},{7,6},{8,9},{9,8},{10,11... | collective-permute-start | bytes 1327112 | tf_op jit(solution)/shard_map/cond/branch_2_fun/ppermute | solution.py:429
  103.1 3.9 %collective-permute-start.83 = (f32[864,128]{1,0:T(8,128)S(1)}, f32[864,128]{1,0:T(8,128)S(1)}, u32[]{:S(2)}, u32[]{:S(2)}) collective-permute-start(f32[864,128]{1,0:T(8,128)S(1)} %get-tuple-element.189), channel_id=1, source_target_pairs={{0,1},{1,0},{2,3},{3,2},{4,5},{5,4},{6,7},{7,6},{8,9},{9,8},{10,11... | collective-permute-start | bytes 1327112 | tf_op jit(solution)/shard_map/cond/branch_2_fun/ppermute | solution.py:429
  103.5 13.0 %collective-permute-start.84 = (f32[864,128]{1,0:T(8,128)S(1)}, f32[864,128]{1,0:T(8,128)S(1)}, u32[]{:S(2)}, u32[]{:S(2)}) collective-permute-start(f32[864,128]{1,0:T(8,128)S(1)} %get-tuple-element.190), channel_id=1, source_target_pairs={{0,2},{1,3},{2,0},{3,1},{4,6},{5,7},{6,4},{7,5},{8,10},{9,11},{10,... | collective-permute-start | bytes 1327112 | tf_op jit(solution)/shard_map/cond/branch_2_fun/ppermute | solution.py:429
  105.0 20.0 %collective-permute-start.85 = (f32[864,128]{1,0:T(8,128)S(1)}, f32[864,128]{1,0:T(8,128)S(1)}, u32[]{:S(2)}, u32[]{:S(2)}) collective-permute-start(f32[864,128]{1,0:T(8,128)S(1)} %get-tuple-element.191), channel_id=1, source_target_pairs={{0,3},{1,2},{2,1},{3,0},{4,7},{5,6},{6,5},{7,4},{8,11},{9,10},{10,... | collective-permute-start | bytes 1327112 | tf_op jit(solution)/shard_map/cond/branch_2_fun/ppermute | solution.py:429
  105.0 20.0 %collective-permute-start.86 = (f32[864,128]{1,0:T(8,128)S(1)}, f32[864,128]{1,0:T(8,128)S(1)}, u32[]{:S(2)}, u32[]{:S(2)}) collective-permute-start(f32[864,128]{1,0:T(8,128)S(1)} %get-tuple-element.192), channel_id=1, source_target_pairs={{0,4},{1,5},{2,6},{3,7},{4,0},{5,1},{6,2},{7,3},{8,12},{9,13},{10,... | collective-permute-start | bytes 1327112 | tf_op jit(solution)/shard_map/cond/branch_2_fun/ppermute | solution.py:429
  106.6 39.4 %collective-permute-start.87 = (f32[864,128]{1,0:T(8,128)S(1)}, f32[864,128]{1,0:T(8,128)S(1)}, u32[]{:S(2)}, u32[]{:S(2)}) collective-permute-start(f32[864,128]{1,0:T(8,128)S(1)} %get-tuple-element.193), channel_id=1, source_target_pairs={{0,5},{1,4},{2,7},{3,6},{4,1},{5,0},{6,3},{7,2},{8,13},{9,12},{10,... | collective-permute-start | bytes 1327112 | tf_op jit(solution)/shard_map/cond/branch_2_fun/ppermute | solution.py:429
  107.0 38.9 %collective-permute-start.88 = (f32[864,128]{1,0:T(8,128)S(1)}, f32[864,128]{1,0:T(8,128)S(1)}, u32[]{:S(2)}, u32[]{:S(2)}) collective-permute-start(f32[864,128]{1,0:T(8,128)S(1)} %get-tuple-element.194), channel_id=1, source_target_pairs={{0,6},{1,7},{2,4},{3,5},{4,2},{5,3},{6,0},{7,1},{8,14},{9,15},{10,... | collective-permute-start | bytes 1327112 | tf_op jit(solution)/shard_map/cond/branch_2_fun/ppermute | solution.py:429
  116.5 29.4 %collective-permute-start.89 = (f32[864,128]{1,0:T(8,128)S(1)}, f32[864,128]{1,0:T(8,128)S(1)}, u32[]{:S(2)}, u32[]{:S(2)}) collective-permute-start(f32[864,128]{1,0:T(8,128)S(1)} %get-tuple-element.195), channel_id=1, source_target_pairs={{0,7},{1,6},{2,5},{3,4},{4,3},{5,2},{6,1},{7,0},{8,15},{9,14},{10,... | collective-permute-start | bytes 1327112 | tf_op jit(solution)/shard_map/cond/branch_2_fun/ppermute | solution.py:429
  147.2 1.2 collective-permute-start.90
  148.4 3.6 %collective-permute-start.91 = (f32[4,4]{1,0:T(4,128)S(1)}, f32[4,4]{1,0:T(4,128)S(1)}, u32[]{:S(2)}, u32[]{:S(2)}) collective-permute-start(f32[4,4]{1,0:T(4,128)S(1)} %add.25), channel_id=1, source_target_pairs={{0,2},{1,3},{2,0},{3,1},{4,6},{5,7},{6,4},{7,5},{8,10},{9,11},{10,... | collective-permute-start | bytes 200 | tf_op jit(solution)/shard_map/cond/branch_2_fun/ppermute | solution.py:429
  152.0 3.6 %collective-permute-start.92 = (f32[4,4]{1,0:T(4,128)S(1)}, f32[4,4]{1,0:T(4,128)S(1)}, u32[]{:S(2)}, u32[]{:S(2)}) collective-permute-start(f32[4,4]{1,0:T(4,128)S(1)} %add.26), channel_id=1, source_target_pairs={{0,4},{1,5},{2,6},{3,7},{4,0},{5,1},{6,2},{7,3},{8,12},{9,13},{10,... | collective-permute-start | bytes 200 | tf_op jit(solution)/shard_map/cond/branch_2_fun/ppermute | solution.py:429
  155.7 1.2 copy-start.3
  155.7 1.2 copy-start.9
